TPU v7x, 1024 devices: a whole 8x8x8 slice. The times are simulated.
1024 devices in a mesh: dp: 16 (over z_lo, y), fsdp: 64 (over x, z_hi, core).
Axes of the slice: x: 8, y: 8, z: 8 (z_hi: 4, z_lo: 2; z = z_hi * 2 + z_lo), core: 2. Of those that a mesh axis runs over, the one named last changes fastest.
Arguments:
- patches: bfloat16 [147456, 6144], P(('dp', 'fsdp')), may hold values from -6 to 6
- labels: int32 [147456], P(('dp', 'fsdp')), may hold values from 0 to 149
- weight: bfloat16 [6144, 150], P('fsdp'), may hold values from -0.21875 to 0.21875
- gain: bfloat16 [6144], P('fsdp'), may hold values from 0.099609375 to 1.8984375
- counts: int32 [4096], P(('dp', 'fsdp')), may hold values from 1 to 36, as said below
- plan: int32 [1024, 2], P(('dp', 'fsdp')), may hold values from 0 to 3, as said below
Outputs:
- logits: bfloat16 [147456, 150], P(('dp', 'fsdp'))
- input_grad: bfloat16 [147456, 6144], P(('dp', 'fsdp'))
- weight_grad: float32 [6144, 150], P('fsdp')
- gain_grad: float32 [6144], P('fsdp')
Inputs may be any that keep to these rules, and one draw needn't show every extreme that they name: `counts`: rows of an image slot at positions from its count on are padding. `plan`: per device, column 0 is the slot whose image goes to the next data group and column 1 the slot whose image goes to the previous one, groups wrapping around; the two columns differ.
All inputs are finite; a program needn't handle non-finite values.
Results may differ from a plain program's by a relative error of at most 0.017.
Values may be sent and summed in bfloat16 or wider, within the bound.
No kernel may reach another device: no remote copies, remote signals or barrier semaphores. Data moves between devices by JAX's collectives and lax.ppermute only.
A program may use at most 64 MiB of HBM per device.

v0:
```python
import math

import jax
import jax.numpy as jnp
from jax import lax
from jax.sharding import PartitionSpec as P


def from_behind(value, axis, steps):
    count = lax.axis_size(axis)
    pairs = [(source, (source + steps) % count) for source in range(count)]
    return lax.ppermute(value, axis, pairs)


def norm_forward(rows32):
    average = jnp.mean(rows32, axis=1, keepdims=True)
    centred = rows32 - average
    inverse = lax.rsqrt(jnp.mean(centred * centred, axis=1, keepdims=True) + 1e-06)
    return (centred * inverse, inverse)


def norm_backward(dact, normed, inverse, gain32):
    dnorm = dact * gain32
    first = jnp.mean(dnorm, axis=1, keepdims=True)
    second = jnp.mean(dnorm * normed, axis=1, keepdims=True)
    return inverse * (dnorm - first - normed * second)


def body(patches, labels, weight, gain, counts, plan):
    total_rows, width = patches.shape
    slot_count = counts.shape[0]
    patch = total_rows // slot_count
    images = patches.reshape(slot_count, patch, width)
    send_up = plan[0, 0]
    send_down = plan[0, 1]
    leave_up = lax.dynamic_index_in_dim(images, send_up, 0, keepdims=False)
    leave_down = lax.dynamic_index_in_dim(images, send_down, 0, keepdims=False)
    count_up = lax.dynamic_slice_in_dim(counts, send_up, 1).astype(jnp.bfloat16)
    count_down = lax.dynamic_slice_in_dim(counts, send_down, 1).astype(jnp.bfloat16)
    arrive_low, length_low = from_behind((leave_up, count_up), "dp", 1)
    arrive_up, length_up = from_behind((leave_down, count_down), "dp", -1)
    full_weight, full_gain = (
        lax.all_gather(weight, "fsdp", axis=0, tiled=True),
        lax.all_gather(gain, "fsdp", axis=0, tiled=True),
    )
    slot_ids = jnp.arange(slot_count, dtype=jnp.int32)
    to_upper = slot_ids == send_up
    to_lower = slot_ids == send_down
    moved = jnp.where(
        to_upper[:, None, None],
        arrive_up[None],
        jnp.where(to_lower[:, None, None], arrive_low[None], images),
    )
    live = jnp.where(
        to_upper,
        length_up.astype(jnp.int32)[0],
        jnp.where(to_lower, length_low.astype(jnp.int32)[0], counts),
    )
    places = jnp.arange(patch, dtype=jnp.int32)
    mask = (places[None, :] < live[:, None]).astype(jnp.float32).reshape(-1, 1)
    gain32 = full_gain.astype(jnp.float32)
    rows32 = moved.reshape(-1, width).astype(jnp.float32)
    normed, inverse = norm_forward(rows32)
    act = (normed * gain32).astype(jnp.bfloat16)
    pre = jnp.dot(act, full_weight, preferred_element_type=jnp.float32)
    shown = (pre * mask).astype(jnp.bfloat16)
    expo = jnp.exp(pre)
    prob = expo / jnp.sum(expo, axis=1, keepdims=True)
    class_ids = jnp.arange(full_weight.shape[1], dtype=jnp.int32)
    onehot = (labels[:, None] == class_ids[None, :]).astype(jnp.float32)
    dpre = (16.0 * (prob - onehot) * mask).astype(jnp.bfloat16)
    dact = lax.dot_general(
        dpre, full_weight, (((1,), (1,)), ((), ())), preferred_element_type=jnp.float32
    )
    input_grad = norm_backward(dact, normed, inverse, gain32).astype(jnp.bfloat16)
    wterm = lax.dot_general(act, dpre, (((0,), (0,)), ((), ())), preferred_element_type=jnp.float32)
    gterm = jnp.sum(dact * normed, axis=0)
    part_w, part_g = (
        lax.psum_scatter(wterm, "fsdp", scatter_dimension=0, tiled=True),
        lax.psum_scatter(gterm, "fsdp", scatter_dimension=0, tiled=True),
    )
    sum_w, sum_g = (
        lax.psum(part_w.astype(jnp.bfloat16), "dp").astype(jnp.float32),
        lax.psum(part_g.astype(jnp.bfloat16), "dp").astype(jnp.float32),
    )
    factor = 1.0 / math.sqrt(total_rows * lax.axis_size("dp") * lax.axis_size("fsdp"))
    return (shown, input_grad, sum_w * factor, sum_g * factor)


def solution(mesh):
    placed = (
        P(("dp", "fsdp"), None),
        P(("dp", "fsdp")),
        P("fsdp", None),
        P("fsdp"),
        P(("dp", "fsdp")),
        P(("dp", "fsdp"), None),
    )
    return jax.shard_map(
        body,
        mesh=mesh,
        in_specs=placed,
        out_specs=(P(("dp", "fsdp"), None), P(("dp", "fsdp"), None), P("fsdp", None), P("fsdp")),
        check_vma=False,
    )
```

profile of v0, /device:TPU:8, one launch (start us, length us, event | category | flops | bytes accessed | tf_op | source)
XLA Modules:
  0.0 713.0 jit_solution(7983417262026928073)
XLA Ops:
  7.2 0.7 all-gather.3.cloned.1.call-update
  8.0 1.3 fusion.22
  13.2 1.3 fusion.21
  15.1 10.2 %collective-permute-start.2 = (bf16[1]{0:T(256)(128)(2,1)}, bf16[1]{0:T(256)(128)(2,1)}, u32[]{:S(2)}, u32[]{:S(2)}) collective-permute-start(bf16[1]{0:T(256)(128)(2,1)} %convert_element_type.54), channel_id=1, source_target_pairs={{0,960},{64,0},{128,64},{192,128},{256,192},{320,256},{384,320},{4... | collective-permute-start | bytes 14 | tf_op jit(solution)/shard_map/ppermute | solution.py:12
  26.0 3.2 collective-permute-start.3
  29.2 1.6 reshape.71
  30.8 0.9 dynamic-slice_bitcast_fusion
  31.7 1.9 collective-permute-start.1
  33.6 6.0 collective-permute-start
  41.3 1.4 fusion.20
  43.6 286.2 %all-reduce = bf16[6144]{0:T(1024)(128)(2,1)S(1)} all-reduce(bf16[6144]{0:T(1024)(128)(2,1)S(1)} %dynamic-update-slice), channel_id=1, replica_groups=mesh['dp'=16,'fsdp'=64] {'fsdp'}, use_global_device_ids=true, to_apply=%add | all-reduce | flops 6144 | bytes 24576
  331.1 1.3 select_select_fusion.1
  333.0 1.4 broadcast_in_dim.64
  334.6 1.4 broadcast_in_dim.69
  336.0 3.6 convert_reduce_fusion
  340.3 3.8 copy.11
  344.1 5.7 reshape.79
  349.8 3.1 exponential_reduce_fusion
  352.9 3.9 fusion.15
  357.3 4.8 fusion.11
  362.1 275.6 %all-reduce.1 = bf16[6144]{0:T(1024)(128)(2,1)S(1)} all-reduce(f32[6144]{0:T(1024)S(1)} %get-tuple-element.4), channel_id=3, replica_groups=mesh['dp'=16,'fsdp'=64] {'fsdp'}, use_global_device_ids=true, to_apply=%region_8.9.clone | all-reduce | flops 6144 | bytes 36864
  637.8 4.5 fusion.10
  642.3 1.0 copy.13
  643.3 61.7 %all-reduce.2 = (bf16[96,150]{0,1:T(8,128)(2,1)S(1)}, bf16[96]{0:T(256)(128)(2,1)S(1)}) all-reduce(bf16[96,150]{0,1:T(8,128)(2,1)S(1)} %copy.13, bf16[96]{0:T(256)(128)(2,1)S(1)} %dynamic-slice.4), channel_id=1, replica_groups=mesh['dp'=16,'fsdp'=64] {'dp'}, use_global_device_ids=true, to_apply=%region_6.7 | all-reduce | flops 14496 | bytes 57984 | tf_op jit(solution)/shard_map/psum | solution.py:83
  (37 shorter events, 4.6 us)
Async XLA Ops:
  7.2 324.0 %copy-start = (s32[4]{0:T(128)S(1)}, s32[4]{0:T(128)}, u32[]{:S(2)}) copy-start(s32[4]{0:T(128)} %param.10) | copy-start | bytes 52
  7.2 36.2 %copy-start.2 = (bf16[96]{0:T(256)(128)(2,1)S(1)}, bf16[96]{0:T(256)(128)(2,1)}, u32[]{:S(2)}) copy-start(bf16[96]{0:T(256)(128)(2,1)} %param.9) | copy-start | bytes 580
  7.2 333.1 %all-gather.3.cloned.1.call-start = ((), (), s32[]{:S(2)}) async-start(), calls=%async_computation.1 | async-start | bytes 2529280 | tf_op jit(solution)/shard_map/all_gather | solution.py:43
  7.9 634.4 %reduce-scatter.4.cloned.1.call-start = ((), (), s32[]{:S(2)}) async-start(), calls=%async_computation.2 | async-start | bytes 6389760
  15.1 314.7 %collective-permute-start.2 = (bf16[1]{0:T(256)(128)(2,1)}, bf16[1]{0:T(256)(128)(2,1)}, u32[]{:S(2)}, u32[]{:S(2)}) collective-permute-start(bf16[1]{0:T(256)(128)(2,1)} %convert_element_type.54), channel_id=1, source_target_pairs={{0,960},{64,0},{128,64},{192,128},{256,192},{320,256},{384,320},{4... | collective-permute-start | bytes 14 | tf_op jit(solution)/shard_map/ppermute | solution.py:12
  26.0 304.5 %collective-permute-start.3 = (bf16[1]{0:T(256)(128)(2,1)}, bf16[1]{0:T(256)(128)(2,1)}, u32[]{:S(2)}, u32[]{:S(2)}) collective-permute-start(bf16[1]{0:T(256)(128)(2,1)} %convert_element_type.55), channel_id=1, source_target_pairs={{0,64},{64,128},{128,192},{192,256},{256,320},{320,384},{384,448},... | collective-permute-start | bytes 14 | tf_op jit(solution)/shard_map/ppermute | solution.py:12
  31.7 302.7 %collective-permute-start.1 = (bf16[36,6144]{1,0:T(8,128)(2,1)S(1)}, bf16[36,6144]{1,0:T(8,128)(2,1)S(1)}, u32[]{:S(2)}, u32[]{:S(2)}) collective-permute-start(bf16[36,6144]{1,0:T(8,128)(2,1)S(1)} %get-tuple-element.11), channel_id=1, source_target_pairs={{0,64},{64,128},{128,192},{192,256},{256,320},{320,384},{384,448},... | collective-permute-start | bytes 1327112 | tf_op jit(solution)/shard_map/ppermute | solution.py:12
  33.6 299.2 %collective-permute-start = (bf16[36,6144]{1,0:T(8,128)(2,1)}, bf16[36,6144]{1,0:T(8,128)(2,1)S(1)}, u32[]{:S(2)}, u32[]{:S(2)}) collective-permute-start(bf16[36,6144]{1,0:T(8,128)(2,1)} %get-tuple-element.12), channel_id=1, source_target_pairs={{0,960},{64,0},{128,64},{192,128},{256,192},{320,256},{384,320},{4... | collective-permute-start | bytes 1327112 | tf_op jit(solution)/shard_map/ppermute | solution.py:12
  349.8 3.1 copy-start.1
Sparse Core Ops, SparseCore 0:
  12.5 107.9 all-gather.2
  356.9 168.4 reduce-scatter.3
where the time goes:
time: 714 us; the launch traced here: 713 us
  blocking collectives  623 us (87%)
  between operations  21.9 us (3%)
  starting transfers between devices  21.4 us (3%)
  local copies, waits for them, and re-layouts  21.1 us (3%)
  other arithmetic  12.7 us (2%)
  matrix products  11.7 us (2%)
    unnamed x2, blocking collectives  562 us
    psum x1, blocking collectives, body(): lax.psum(part_w.astype(jnp.bfloat16), 'dp').astype(jnp.float32)  61.7 us
    ppermute x4, starting transfers between devices, from_behind(): return lax.ppermute(value, axis, pairs)  21.3 us
  transfers between devices with their start and end apart: 6, of which 0 were waited for; matrix products, arithmetic and copies ran while one was open for 4% of the time, Pallas kernels for 0%

commit v1 on v0

v1 whole, which is shorter than its diff:
```python
import math

import jax
import jax.numpy as jnp
from jax import lax
from jax.sharding import Mesh
from jax.sharding import PartitionSpec as P

Z_LO, Y, X, Z_HI, CORE = 2, 8, 8, 4, 2
NAMES = ("z_lo", "y", "x", "z_hi", "core")
DATA = ("z_lo", "y")
PLANE = ("x", "z_hi")
CUBE = ("z_lo", "x", "z_hi")
PAD = 160


def from_behind(value, axes, steps):
    count = lax.axis_size(axes)
    pairs = [(source, (source + steps) % count) for source in range(count)]
    return lax.ppermute(value, axes, pairs)


def send_to_all(value, axes):
    count = lax.axis_size(axes)
    copies = jnp.broadcast_to(value[None], (count,) + value.shape)
    return lax.all_to_all(copies, axes, 0, 0)


def move(patches, counts, plan):
    total_rows, width = patches.shape
    slot_count = counts.shape[0]
    patch = total_rows // slot_count
    images = patches.reshape(slot_count, patch, width)
    up, down = plan[0, 0], plan[0, 1]

    def parcel(slot):
        image = lax.dynamic_index_in_dim(images, slot, 0, keepdims=False)
        count = lax.dynamic_slice_in_dim(counts, slot, 1).astype(jnp.bfloat16)
        return jnp.concatenate([image, jnp.broadcast_to(count[:, None], (1, width))])

    arrive_low = from_behind(parcel(up), DATA, 1)
    arrive_up = from_behind(parcel(down), DATA, -1)
    slot_ids = jnp.arange(slot_count, dtype=jnp.int32)
    to_upper = slot_ids == up
    to_lower = slot_ids == down
    moved = jnp.where(
        to_upper[:, None, None],
        arrive_up[None, :patch],
        jnp.where(to_lower[:, None, None], arrive_low[None, :patch], images),
    )
    live = jnp.where(
        to_upper,
        arrive_up[patch, 0].astype(jnp.int32),
        jnp.where(to_lower, arrive_low[patch, 0].astype(jnp.int32), counts),
    )
    places = jnp.arange(patch, dtype=jnp.int32)
    mask = (places[None, :] < live[:, None]).astype(jnp.float32).reshape(-1, 1)
    return moved.reshape(-1, width), mask


def body(patches, labels, weight, gain, counts, plan):
    total_rows, width = patches.shape
    share, classes = weight.shape
    gain32 = gain.astype(jnp.float32)[:, None]
    scaled = (weight.astype(jnp.float32) * gain32).astype(jnp.bfloat16)
    scaled = jnp.pad(scaled.T, ((0, PAD - classes), (0, 0)))
    rows, mask = move(patches, counts, plan)
    plane = send_to_all(scaled, PLANE)
    both = lax.all_gather(plane, "core")
    full = both.transpose(2, 1, 0, 3).reshape(PAD, width)

    rows32 = rows.astype(jnp.float32)
    average = jnp.mean(rows32, axis=1, keepdims=True)
    centred = rows32 - average
    inverse = lax.rsqrt(jnp.mean(centred * centred, axis=1, keepdims=True) + 1e-06)
    normed = centred * inverse
    act = normed.astype(jnp.bfloat16)
    pre = lax.dot_general(act, full, (((1,), (1,)), ((), ())), preferred_element_type=jnp.float32)
    class_ids = jnp.arange(PAD, dtype=jnp.int32)[None, :]
    expo = jnp.where(class_ids < classes, jnp.exp(pre), 0.0)
    prob = expo / jnp.sum(expo, axis=1, keepdims=True)
    onehot = (labels[:, None] == class_ids).astype(jnp.float32)
    dpre = (16.0 * (prob - onehot) * mask).astype(jnp.bfloat16)
    shown = (pre * mask)[:, :classes].astype(jnp.bfloat16)

    term = lax.dot_general(dpre, act, (((0,), (0,)), ((), ())), preferred_element_type=jnp.float32)
    blocks = term.astype(jnp.bfloat16).reshape(Z_LO, PAD // Z_LO, X, Z_HI, CORE, share)
    blocks = blocks.transpose(4, 0, 2, 3, 1, 5).reshape(CORE, Z_LO * X * Z_HI, PAD // Z_LO, share)
    core = lax.axis_index("core")
    mine = lax.dynamic_index_in_dim(blocks, core, 0, keepdims=False)
    other = lax.dynamic_index_in_dim(blocks, 1 - core, 0, keepdims=False)
    other = from_behind(other, "core", 1)
    chip = (mine.astype(jnp.float32) + other.astype(jnp.float32)).astype(jnp.bfloat16)

    dnorm = jnp.dot(dpre, full, preferred_element_type=jnp.float32)
    first = jnp.mean(dnorm, axis=1, keepdims=True)
    second = jnp.mean(dnorm * normed, axis=1, keepdims=True)
    input_grad = (inverse * (dnorm - first - normed * second)).astype(jnp.bfloat16)

    cube = lax.all_to_all(chip, CUBE, 0, 0)
    cube = jnp.sum(cube.astype(jnp.float32), axis=0).astype(jnp.bfloat16)
    group = send_to_all(cube, DATA).reshape(Z_LO, Y, PAD // Z_LO, share)
    total = jnp.sum(group.astype(jnp.float32), axis=1).reshape(PAD, share)[:classes].T
    factor = 1.0 / math.sqrt(total_rows * Z_LO * Y * X * Z_HI * CORE)
    weight_grad = total * (gain32 * factor)
    gain_grad = jnp.sum(weight.astype(jnp.float32) * total, axis=1) * factor
    return (shown, input_grad, weight_grad, gain_grad)


def solution(mesh):
    fine = Mesh(mesh.devices.reshape(Z_LO, Y, X, Z_HI, CORE), NAMES)
    shards = ("x", "z_hi", "core")
    placed = (P(NAMES, None), P(NAMES), P(shards, None), P(shards), P(NAMES), P(NAMES, None))
    return jax.shard_map(
        body,
        mesh=fine,
        in_specs=placed,
        out_specs=(P(NAMES, None), P(NAMES, None), P(shards, None), P(shards)),
        check_vma=False,
    )
```

time: 714 us -> 208 us (0.29)
  the two profiles are of different devices: /device:TPU:8 before, /device:TPU:18 now
where the time goes in v1:
time: 208 us; the launch traced here: 207 us
  waiting for transfers between devices  71.1 us (34%)
  starting transfers between devices  51.5 us (25%)
  local copies, waits for them, and re-layouts  36.3 us (17%)
  between operations  20.8 us (10%)
  other arithmetic  18 us (9%)
  matrix products  9 us (4%)
    all_to_all x1, waiting for transfers between devices, body(): cube = lax.all_to_all(chip, CUBE, 0, 0)  30.9 us
    all_to_all x2, starting transfers between devices, send_to_all(): return lax.all_to_all(copies, axes, 0, 0)  29.3 us
    all_to_all x2, waiting for transfers between devices, send_to_all(): return lax.all_to_all(copies, axes, 0, 0)  24.3 us
    all_to_all x1, starting transfers between devices, body(): cube = lax.all_to_all(chip, CUBE, 0, 0)  14 us
    all_gather x1, waiting for transfers between devices, body(): both = lax.all_gather(plane, 'core')  13 us
    reshape x2, local copies, waits for them, and re-layouts, body(): term.astype(jnp.bfloat16).reshape(Z_LO, PAD // Z_LO, X, Z_HI, CORE, share)  8.56 us
    ppermute x3, starting transfers between devices, from_behind(): return lax.ppermute(value, axes, pairs)  8.04 us
    reshape x1, local copies, waits for them, and re-layouts, body(): full = both.transpose(2, 1, 0, 3).reshape(PAD, width)  5.99 us
  transfers between devices with their start and end apart: 7, of which 5 were waited for; matrix products, arithmetic and copies ran while one was open for 13% of the time, Pallas kernels for 0%

profile of v1, /device:TPU:18, one launch (start us, length us, event | category | flops | bytes accessed | tf_op | source)
XLA Modules:
  0.0 206.7 jit_solution(17883294975579101268)
XLA Ops:
  10.0 21.4 %all-to-all-start = ((bf16[32,160,96]{2,1,0:T(8,128)(2,1)}), bf16[32,160,96]{2,1,0:T(8,128)(2,1)S(1)}, u32[]{:S(2)}, u32[]{:S(2)}) async-start(bf16[32,160,96]{2,1,0:T(8,128)(2,1)} %broadcast_in_dim.107), calls=%async_computation | async-start | bytes 2621440 | tf_op jit(solution)/shard_map/all_to_all | solution.py:26
  37.3 1.5 reshape.107
  40.1 2.2 %collective-permute-start = (bf16[37,6144]{1,0:T(8,128)(2,1)S(1)}, bf16[37,6144]{1,0:T(8,128)(2,1)S(1)}, u32[]{:S(2)}, u32[]{:S(2)}) collective-permute-start(bf16[37,6144]{1,0:T(8,128)(2,1)S(1)} %concatenate.6), channel_id=1, source_target_pairs={{0,960},{64,0},{128,64},{192,128},{256,192},{320,256},{384,320},{4... | collective-permute-start | bytes 1363976 | tf_op jit(solution)/shard_map/ppermute | solution.py:20
  43.1 3.6 %collective-permute-start.1 = (bf16[37,6144]{1,0:T(8,128)(2,1)S(1)}, bf16[37,6144]{1,0:T(8,128)(2,1)S(1)}, u32[]{:S(2)}, u32[]{:S(2)}) collective-permute-start(bf16[37,6144]{1,0:T(8,128)(2,1)S(1)} %concatenate.7), channel_id=1, source_target_pairs={{0,64},{64,128},{128,192},{192,256},{256,320},{320,384},{384,448},... | collective-permute-start | bytes 1363976 | tf_op jit(solution)/shard_map/ppermute | solution.py:20
  46.7 19.5 %all-to-all-done = bf16[32,160,96]{2,1,0:T(8,128)(2,1)S(1)} async-done(((bf16[32,160,96]{2,1,0:T(8,128)(2,1)}), bf16[32,160,96]{2,1,0:T(8,128)(2,1)S(1)}, u32[]{:S(2)}, u32[]{:S(2)}) %all-to-all-start) | async-done | bytes 983072 | tf_op jit(solution)/shard_map/all_to_all | solution.py:26
  74.1 1.5 broadcast_in_dim.106
  77.2 3.6 %convert_reduce_fusion = (f32[144]{0:T(256)S(1)}, bf16[144,6144]{1,0:T(8,128)(2,1)S(1)}) fusion(bf16[144,6144]{1,0:T(8,128)(2,1)} %broadcast_in_dim.100, bf16[144,6144]{1,0:T(8,128)(2,1)} %broadcast_in_dim.106, bf16[144,6144]{1,0:T(8,128)(2,1)} %param.6, pred[144]{0:T(512)(128)(4,1)S(1)} %broadcast_in_dim.102, pred[144]{0:T(512)(128)(4,1)S(1)} %broadcast_in_dim.96), kind=kLoop, calls=%fused_computation.2 | loop fusion | flops 3538800 | bytes 7078752 | tf_op jit(solution)/shard_map/reduce_sum | solution.py:73
  81.5 13.0 %all-gather.3.cloned.1.call-done = bf16[64,160,96]{2,1,0:T(8,128)(2,1)} async-done(((bf16[32,160,96]{2,1,0:T(8,128)(2,1)}), bf16[64,160,96]{2,1,0:T(8,128)(2,1)}) %all-gather.3.cloned.1.call-update) | async-done | bytes 1966096 | tf_op jit(solution)/shard_map/all_gather | solution.py:69
  94.5 5.9 %copy.15 = bf16[160,32,2,96]{3,2,1,0:T(2,128)(2,1)} copy(bf16[160,32,2,96]{3,0,1,2:T(8,128)(2,1)} %bitcast.41) | data formatting | bytes 3932160 | tf_op jit(solution)/shard_map/transpose | solution.py:70
  100.5 6.0 %reshape.108 = bf16[160,6144]{1,0:T(8,128)(2,1)} reshape(bf16[160,32,2,96]{3,2,1,0:T(2,128)(2,1)} %copy.15) | data formatting | bytes 3932160 | tf_op jit(solution)/shard_map/reshape | solution.py:70
  106.5 2.4 %fusion.12 = (f32[144]{0:T(256)S(1)}, f32[144,160]{1,0:T(8,128)S(1)}) fusion(pred[160]{0:T(512)(128)(4,1)S(1)} %iota_compare_fusion.2, bf16[160,6144]{1,0:T(8,128)(2,1)} %reshape.108, bf16[144,6144]{1,0:T(8,128)(2,1)S(1)} %get-tuple-element.7, f32[144]{0:T(256)S(1)} %add_rsqrt_fusion, f32[144]{0:T(256)S(1)} %broadcast_multiply_fusion.2), kind=kOutput, calls=%fused_computation.25 | convolution fusion | flops 286700416 | bytes 3829600 | tf_op jit(solution)/shard_map/dot_general | solution.py:78
  108.9 2.1 %convolution_convert_fusion = bf16[160,6144]{1,0:T(8,128)(2,1)} fusion(f32[144,160]{1,0:T(8,128)S(1)} %get-tuple-element.17, f32[144]{0:T(256)S(1)} %mul.91, s32[144]{0:T(256)S(1)} %copy-done.9, f32[144]{0:T(256)S(1)} %get-tuple-element.16, pred[160]{0:T(512)(128)(4,1)S(1)} %iota_compare_fusion.2, bf16[144,6144]{1,0:T(8,128)(2,1)S(1)} %get-tuple-element.7, ...), kind=kOutput, calls=%fused_computation | convolution fusion | flops 287798784 | bytes 3830752 | tf_op jit(solution)/shard_map/dot_general | solution.py:86
  111.0 5.1 %reshape.109 = bf16[2,80,8,4,2,96]{5,4,3,2,1,0:T(2,128)(2,1)} reshape(bf16[160,6144]{1,0:T(8,128)(2,1)} %convolution_convert_fusion) | data formatting | bytes 3932160 | tf_op jit(solution)/shard_map/reshape | solution.py:87
  116.2 3.4 %copy.16 = bf16[2,80,8,4,2,96]{5,1,3,2,0,4:T(8,128)(2,1)S(1)} copy(bf16[2,80,8,4,2,96]{5,4,3,2,1,0:T(2,128)(2,1)} %reshape.109) | data formatting | bytes 3932160 | tf_op jit(solution)/shard_map/reshape | solution.py:87
  119.6 1.5 copy-done
  122.2 2.2 %collective-permute-start.2 = (bf16[64,80,96]{2,1,0:T(8,128)(2,1)}, bf16[64,80,96]{2,1,0:T(8,128)(2,1)S(1)}, u32[]{:S(2)}, u32[]{:S(2)}) collective-permute-start(bf16[64,80,96]{2,1,0:T(8,128)(2,1)} %dynamic-slice_bitcast_fusion), channel_id=1, source_target_pairs={{0,1},{1,0},{2,3},{3,2},{4,5},{5,4},{6,7},{7,6},{8,9},{9,8},{10,11... | collective-permute-start | bytes 2949128 | tf_op jit(solution)/shard_map/ppermute | solution.py:20
  124.4 2.9 %collective-permute-done.2 = bf16[64,80,96]{2,1,0:T(8,128)(2,1)S(1)} collective-permute-done((bf16[64,80,96]{2,1,0:T(8,128)(2,1)}, bf16[64,80,96]{2,1,0:T(8,128)(2,1)S(1)}, u32[]{:S(2)}, u32[]{:S(2)}) %collective-permute-start.2) | collective-permute-done | bytes 983072 | tf_op jit(solution)/shard_map/ppermute | solution.py:20
  127.3 2.7 %fusion.10 = bf16[64,80,96]{2,1,0:T(8,128)(2,1)} fusion(bf16[64,80,96]{2,1,0:T(8,128)(2,1)S(1)} %collective-permute-done.2, bf16[2,64,80,96]{3,2,1,0:T(8,128)(2,1)} %bitcast.40, s32[]{:T(128)S(6)} %select_n.43), kind=kLoop, calls=%fused_computation.14 | loop fusion | flops 1966080 | bytes 2949124 | tf_op jit(solution)/shard_map/convert_element_type | solution.py:93
  130.0 14.0 %all-to-all-start.1 = ((bf16[64,80,96]{2,1,0:T(8,128)(2,1)}), bf16[64,80,96]{2,1,0:T(8,128)(2,1)S(1)}, u32[]{:S(2)}, u32[]{:S(2)}) async-start(bf16[64,80,96]{2,1,0:T(8,128)(2,1)} %fusion.10), calls=%async_computation.1 | async-start | bytes 2621440 | tf_op jit(solution)/shard_map/all_to_all | solution.py:100
  144.3 4.4 %fusion.23 = (f32[144]{0:T(256)S(1)}, f32[144]{0:T(256)S(1)}, f32[144,6144]{1,0:T(8,128)}) fusion(f32[144]{0:T(256)S(1)} %add_rsqrt_fusion, f32[144]{0:T(256)S(1)} %broadcast_multiply_fusion.2, bf16[144,6144]{1,0:T(8,128)(2,1)S(1)} %get-tuple-element.7, bf16[160,6144]{1,0:T(8,128)(2,1)} %reshape.108, f32[144,160]{1,0:T(8,128)S(1)} %get-tuple-element.17, ...), kind=kOutput, calls=%fused_computation.48 | convolution fusion | flops 288584960 | bytes 7370848 | tf_op jit(solution)/shard_map/dot_general | solution.py:95
  148.7 30.9 %all-to-all-done.1 = bf16[64,80,96]{2,1,0:T(8,128)(2,1)S(1)} async-done(((bf16[64,80,96]{2,1,0:T(8,128)(2,1)}), bf16[64,80,96]{2,1,0:T(8,128)(2,1)S(1)}, u32[]{:S(2)}, u32[]{:S(2)}) %all-to-all-start.1) | async-done | bytes 983072 | tf_op jit(solution)/shard_map/all_to_all | solution.py:100
  180.7 8.0 %all-to-all-start.2 = ((bf16[16,80,96]{2,1,0:T(8,128)(2,1)}), bf16[16,80,96]{2,1,0:T(8,128)(2,1)S(1)}, u32[]{:S(2)}, u32[]{:S(2)}) async-start(bf16[16,80,96]{2,1,0:T(8,128)(2,1)} %broadcast_in_dim.112), calls=%async_computation.2 | async-start | bytes 655360 | tf_op jit(solution)/shard_map/all_to_all | solution.py:26
  188.6 4.4 %fusion.8 = bf16[144,6144]{1,0:T(8,128)(2,1)} fusion(bf16[144,6144]{1,0:T(8,128)(2,1)S(1)} %get-tuple-element.7, f32[144,6144]{1,0:T(8,128)} %get-tuple-element.18, f32[144]{0:T(256)S(1)} %get-tuple-element.19, f32[144]{0:T(256)S(1)} %get-tuple-element.20, f32[144]{0:T(256)S(1)} %add_rsqrt_fusion, f32[144]{0:T(256)S(1)} %broadcast_multiply_fusion.2), kind=kLoop, calls=%fused_computation.11 | loop fusion | flops 7077888 | bytes 7080192 | tf_op jit(solution)/shard_map/convert_element_type | solution.py:98
  193.8 4.8 %all-to-all-done.2 = bf16[16,80,96]{2,1,0:T(8,128)(2,1)S(1)} async-done(((bf16[16,80,96]{2,1,0:T(8,128)(2,1)}), bf16[16,80,96]{2,1,0:T(8,128)(2,1)S(1)}, u32[]{:S(2)}, u32[]{:S(2)}) %all-to-all-start.2) | async-done | bytes 245792 | tf_op jit(solution)/shard_map/all_to_all | solution.py:26
  (63 shorter events, 18.6 us)
Async XLA Ops:
  7.2 24.3 %copy-start.8 = (s32[1,2]{1,0:T(1,128)S(1)}, s32[1,2]{1,0:T(1,128)}, u32[]{:S(2)}) copy-start(s32[1,2]{1,0:T(1,128)} %param.11) | copy-start | bytes 28
  7.2 28.8 %copy-start.7 = (s32[4]{0:T(128)S(1)}, s32[4]{0:T(128)}, u32[]{:S(2)}) copy-start(s32[4]{0:T(128)} %param.10) | copy-start | bytes 52
  7.2 30.1 %copy-start.1 = (bf16[144,6144]{1,0:T(8,128)(2,1)S(1)}, bf16[144,6144]{1,0:T(8,128)(2,1)}, u32[]{:S(2)}) copy-start(bf16[144,6144]{1,0:T(8,128)(2,1)} %param.6) | copy-start | bytes 5308420
  10.0 56.1 %all-to-all-start = ((bf16[32,160,96]{2,1,0:T(8,128)(2,1)}), bf16[32,160,96]{2,1,0:T(8,128)(2,1)S(1)}, u32[]{:S(2)}, u32[]{:S(2)}) async-start(bf16[32,160,96]{2,1,0:T(8,128)(2,1)} %broadcast_in_dim.107), calls=%async_computation | async-start | bytes 2621440 | tf_op jit(solution)/shard_map/all_to_all | solution.py:26
  31.4 63.1 %all-gather.3.cloned.1.call-start = ((), (), s32[]{:S(2)}) async-start(), calls=%async_computation.3 | async-start | bytes 3932160 | tf_op jit(solution)/shard_map/all_gather | solution.py:69
  40.1 28.8 %collective-permute-start = (bf16[37,6144]{1,0:T(8,128)(2,1)S(1)}, bf16[37,6144]{1,0:T(8,128)(2,1)S(1)}, u32[]{:S(2)}, u32[]{:S(2)}) collective-permute-start(bf16[37,6144]{1,0:T(8,128)(2,1)S(1)} %concatenate.6), channel_id=1, source_target_pairs={{0,960},{64,0},{128,64},{192,128},{256,192},{320,256},{384,320},{4... | collective-permute-start | bytes 1363976 | tf_op jit(solution)/shard_map/ppermute | solution.py:20
  43.1 27.1 %collective-permute-start.1 = (bf16[37,6144]{1,0:T(8,128)(2,1)S(1)}, bf16[37,6144]{1,0:T(8,128)(2,1)S(1)}, u32[]{:S(2)}, u32[]{:S(2)}) collective-permute-start(bf16[37,6144]{1,0:T(8,128)(2,1)S(1)} %concatenate.7), channel_id=1, source_target_pairs={{0,64},{64,128},{128,192},{192,256},{256,320},{320,384},{384,448},... | collective-permute-start | bytes 1363976 | tf_op jit(solution)/shard_map/ppermute | solution.py:20
  66.2 1.1 copy-start.2
  68.9 3.9 %copy-start.3 = (bf16[37,6144]{1,0:T(8,128)(2,1)}, bf16[37,6144]{1,0:T(8,128)(2,1)S(1)}, u32[]{:S(2)}) copy-start(bf16[37,6144]{1,0:T(8,128)(2,1)S(1)} %collective-permute-done) | copy-start | bytes 1363972
  70.1 2.7 %copy-start.5 = (bf16[37,6144]{1,0:T(8,128)(2,1)}, bf16[37,6144]{1,0:T(8,128)(2,1)S(1)}, u32[]{:S(2)}) copy-start(bf16[37,6144]{1,0:T(8,128)(2,1)S(1)} %collective-permute-done.1) | copy-start | bytes 1363972
  72.8 2.8 %copy-start.4 = (bf16[37,6144]{1,0:T(8,128)(2,1)S(1)}, bf16[37,6144]{1,0:T(8,128)(2,1)}, u32[]{:S(2)}) copy-start(bf16[37,6144]{1,0:T(8,128)(2,1)} %copy-done.3) | copy-start | bytes 1363972
  106.5 2.4 %copy-start.9 = (s32[144]{0:T(256)S(1)}, s32[144]{0:T(256)}, u32[]{:S(2)}) copy-start(s32[144]{0:T(256)} %param.7) | copy-start | bytes 1732
  119.6 1.5 copy-start
  122.2 5.1 %collective-permute-start.2 = (bf16[64,80,96]{2,1,0:T(8,128)(2,1)}, bf16[64,80,96]{2,1,0:T(8,128)(2,1)S(1)}, u32[]{:S(2)}, u32[]{:S(2)}) collective-permute-start(bf16[64,80,96]{2,1,0:T(8,128)(2,1)} %dynamic-slice_bitcast_fusion), channel_id=1, source_target_pairs={{0,1},{1,0},{2,3},{3,2},{4,5},{5,4},{6,7},{7,6},{8,9},{9,8},{10,11... | collective-permute-start | bytes 2949128 | tf_op jit(solution)/shard_map/ppermute | solution.py:20
  124.4 19.7 %copy-start.10 = (bf16[96]{0:T(256)(128)(2,1)S(1)}, bf16[96]{0:T(256)(128)(2,1)}, u32[]{:S(2)}) copy-start(bf16[96]{0:T(256)(128)(2,1)} %param.9) | copy-start | bytes 580
  130.0 49.6 %all-to-all-start.1 = ((bf16[64,80,96]{2,1,0:T(8,128)(2,1)}), bf16[64,80,96]{2,1,0:T(8,128)(2,1)S(1)}, u32[]{:S(2)}, u32[]{:S(2)}) async-start(bf16[64,80,96]{2,1,0:T(8,128)(2,1)} %fusion.10), calls=%async_computation.1 | async-start | bytes 2621440 | tf_op jit(solution)/shard_map/all_to_all | solution.py:100
  180.7 17.9 %all-to-all-start.2 = ((bf16[16,80,96]{2,1,0:T(8,128)(2,1)}), bf16[16,80,96]{2,1,0:T(8,128)(2,1)S(1)}, u32[]{:S(2)}, u32[]{:S(2)}) async-start(bf16[16,80,96]{2,1,0:T(8,128)(2,1)} %broadcast_in_dim.112), calls=%async_computation.2 | async-start | bytes 655360 | tf_op jit(solution)/shard_map/all_to_all | solution.py:26
  188.6 10.0 %copy-start.6 = (bf16[96,150]{0,1:T(8,128)(2,1)S(1)}, bf16[96,150]{0,1:T(8,128)(2,1)}, u32[]{:S(2)}) copy-start(bf16[96,150]{0,1:T(8,128)(2,1)} %param.8) | copy-start | bytes 86404
Sparse Core Ops, SparseCore 0:
  67.4 27.1 all-gather.2

commit v2 on v1

v2 whole, which is shorter than its diff:
```python
import math

import jax
import jax.numpy as jnp
from jax import lax
from jax.experimental import pallas as pl
from jax.experimental.pallas import tpu as pltpu
from jax.sharding import Mesh
from jax.sharding import PartitionSpec as P

Z_LO, Y, X, Z_HI, CORE = 2, 8, 8, 4, 2
NAMES = ("z_lo", "y", "x", "z_hi", "core")
DATA = ("z_lo", "y")
PLANE = ("x", "z_hi")
GROUPS, STEP, SHARE = 4, 40, 96
LANES = GROUPS * SHARE
SLOT = 48
INNER = GROUPS * SLOT


def from_behind(value, axes, steps):
    count = lax.axis_size(axes)
    pairs = [(source, (source + steps) % count) for source in range(count)]
    return lax.ppermute(value, axes, pairs)


def vmem_call(kernel, shapes, cost, *operands, scalars=0):
    specs = [
        pl.BlockSpec(memory_space=pltpu.SMEM if place < scalars else pltpu.VMEM)
        for place in range(len(operands))
    ]
    return pl.pallas_call(
        kernel,
        out_shape=shapes,
        in_specs=specs,
        out_specs=[pl.BlockSpec(memory_space=pltpu.VMEM)] * len(shapes),
        compiler_params=pltpu.CompilerParams(vmem_limit_bytes=32 * 1024 * 1024),
        cost_estimate=pl.CostEstimate(flops=cost[0], bytes_accessed=cost[1], transcendentals=0),
    )(*operands)


def prepare_kernel(weight_ref, gain_ref, out_ref):
    classes = weight_ref.shape[0]
    scaled = weight_ref[...].astype(jnp.float32) * gain_ref[...].astype(jnp.float32)
    scaled = jnp.concatenate(
        [scaled, jnp.zeros((GROUPS * STEP - classes, SHARE), jnp.float32)], axis=0
    )
    parts = [scaled[STEP * g : STEP * (g + 1)] for g in range(GROUPS)]
    parcel = jnp.concatenate(parts, axis=1).astype(jnp.bfloat16)
    for place in range(out_ref.shape[0]):
        out_ref[place] = parcel


def main_kernel(
    core_ref, act_ref, own_ref, partner_ref, labels_ref, mask_ref, ids_ref,
    shown_ref, dpre_ref, full_ref, keep_ref, send_ref,
):
    first = core_ref[0] == 0
    count, classes = own_ref.shape[0], shown_ref.shape[1]
    for g in range(GROUPS):
        full_ref[SLOT * g : SLOT * (g + 1)] = jnp.zeros((SLOT, full_ref.shape[1]), jnp.bfloat16)

    for q in range(count // 2):
        shards = []
        for p in (2 * q, 2 * q + 1):
            own, partner = own_ref[p], partner_ref[p]
            shards.append(jnp.where(first, own, partner))
            shards.append(jnp.where(first, partner, own))
        for g in range(GROUPS):
            row = [shard[:, SHARE * g : SHARE * (g + 1)] for shard in shards]
            full_ref[SLOT * g : SLOT * g + STEP, LANES * q : LANES * (q + 1)] = jnp.concatenate(row, axis=1)

    pre = lax.dot_general(
        act_ref[...], full_ref[...], (((1,), (1,)), ((), ())), preferred_element_type=jnp.float32
    )
    ids = ids_ref[...]
    mask = mask_ref[...]
    expo = jnp.where(ids >= 0, jnp.exp(pre), 0.0)
    prob = expo / jnp.sum(expo, axis=1, keepdims=True)
    onehot = jnp.where(labels_ref[...] == ids, 1.0, 0.0)
    dpre32 = 16.0 * (prob - onehot) * mask
    dpre_ref[...] = dpre32.astype(jnp.bfloat16)
    shown = pre * mask
    parts = [shown[:, SLOT * g : SLOT * g + STEP] for g in range(GROUPS)]
    shown_ref[...] = jnp.concatenate(parts, axis=1)[:, :classes].astype(jnp.bfloat16)

    turned = dpre32.T.astype(jnp.bfloat16)
    for q in range(count // 2):
        term = jnp.dot(
            turned, act_ref[:, LANES * q : LANES * (q + 1)], preferred_element_type=jnp.float32
        ).astype(jnp.bfloat16)
        groups = [term[SLOT * g : SLOT * g + STEP] for g in range(GROUPS)]
        shards = [
            jnp.concatenate([group[:, SHARE * k : SHARE * (k + 1)] for group in groups], axis=1)
            for k in range(4)
        ]
        for half in range(2):
            even, odd = shards[2 * half], shards[2 * half + 1]
            keep_ref[2 * q + half] = jnp.where(first, even, odd)
            send_ref[2 * q + half] = jnp.where(first, odd, even)


def move(patches, counts, plan):
    total_rows, width = patches.shape
    slot_count = counts.shape[0]
    patch = total_rows // slot_count
    up, down = plan[0, 0], plan[0, 1]

    def parcel(slot):
        image = lax.dynamic_slice(patches, (slot * patch, 0), (patch, width))
        count = lax.dynamic_slice_in_dim(counts, slot, 1).astype(jnp.bfloat16)
        return jnp.concatenate([image, jnp.broadcast_to(count[:, None], (1, width))])

    arrive_low = from_behind(parcel(up), DATA, 1)
    arrive_up = from_behind(parcel(down), DATA, -1)
    rows = lax.dynamic_update_slice(patches, arrive_low[:patch], (down * patch, 0))
    rows = lax.dynamic_update_slice(rows, arrive_up[:patch], (up * patch, 0))
    slot_ids = jnp.arange(slot_count, dtype=jnp.int32)
    live = jnp.where(
        slot_ids == up,
        arrive_up[patch, 0].astype(jnp.int32),
        jnp.where(slot_ids == down, arrive_low[patch, 0].astype(jnp.int32), counts),
    )
    places = jnp.arange(patch, dtype=jnp.int32)
    mask = (places[None, :] < live[:, None]).astype(jnp.float32).reshape(-1, 1)
    return rows, mask


def body(patches, labels, weight, gain, counts, plan):
    total_rows, width = patches.shape
    share, classes = weight.shape
    peers = X * Z_HI
    core = lax.axis_index("core").astype(jnp.int32)
    wire = jax.ShapeDtypeStruct((peers, STEP, LANES), jnp.bfloat16)
    (copies,) = vmem_call(prepare_kernel, [wire], (0, 2**20), weight.T, gain[None, :])
    plane = lax.all_to_all(copies, PLANE, 0, 0)

    rows, mask = move(patches, counts, plan)
    rows32 = rows.astype(jnp.float32)
    average = jnp.mean(rows32, axis=1, keepdims=True)
    centred = rows32 - average
    inverse = lax.rsqrt(jnp.mean(centred * centred, axis=1, keepdims=True) + 1e-06)
    normed = centred * inverse
    act = normed.astype(jnp.bfloat16)

    partner = from_behind(plane, "core", 1)
    slots = jnp.arange(INNER, dtype=jnp.int32)
    ids = (slots // SLOT) * STEP + slots % SLOT
    ids = jnp.where((slots % SLOT < STEP) & (ids < classes), ids, -1)[None, :]
    shown, dpre, full, keep, send = vmem_call(
        main_kernel,
        [
            jax.ShapeDtypeStruct((total_rows, classes), jnp.bfloat16),
            jax.ShapeDtypeStruct((total_rows, INNER), jnp.bfloat16),
            jax.ShapeDtypeStruct((INNER, width), jnp.bfloat16),
            wire,
            wire,
        ],
        (4 * total_rows * width * INNER, 12 * 2**20),
        core[None], act, plane, partner, labels[:, None], mask, ids,
        scalars=1,
    )
    other = from_behind(send, "core", 1)
    chip = (keep.astype(jnp.float32) + other.astype(jnp.float32)).astype(jnp.bfloat16)

    dnorm = jnp.dot(dpre, full, preferred_element_type=jnp.float32)
    first = jnp.mean(dnorm, axis=1, keepdims=True)
    second = jnp.mean(dnorm * normed, axis=1, keepdims=True)
    input_grad = (inverse * (dnorm - first - normed * second)).astype(jnp.bfloat16)

    owned = lax.all_to_all(chip, PLANE, 0, 0)
    owned = jnp.sum(owned.astype(jnp.float32), axis=0).astype(jnp.bfloat16)
    group = jnp.broadcast_to(owned[None], (Z_LO * Y,) + owned.shape)
    group = lax.all_to_all(group, DATA, 0, 0)
    total = jnp.sum(group.astype(jnp.float32), axis=0)
    total = total.reshape(STEP, GROUPS, share).transpose(1, 0, 2).reshape(GROUPS * STEP, share)
    total = total[:classes]
    factor = 1.0 / math.sqrt(total_rows * Z_LO * Y * X * Z_HI * CORE)
    gain32 = gain.astype(jnp.float32)[None, :]
    weight_grad = (total * (gain32 * factor)).T
    gain_grad = jnp.sum(weight.T.astype(jnp.float32) * total, axis=0) * factor
    return (shown, input_grad, weight_grad, gain_grad)


def solution(mesh):
    fine = Mesh(mesh.devices.reshape(Z_LO, Y, X, Z_HI, CORE), NAMES)
    shards = ("x", "z_hi", "core")
    placed = (P(NAMES, None), P(NAMES), P(shards, None), P(shards), P(NAMES), P(NAMES, None))
    return jax.shard_map(
        body,
        mesh=fine,
        in_specs=placed,
        out_specs=(P(NAMES, None), P(NAMES, None), P(shards, None), P(shards)),
        check_vma=False,
    )
```

time: 208 us -> 145 us (0.70)
  the two profiles are of different devices: /device:TPU:18 before, /device:TPU:16 now
where the time goes in v2:
time: 145 us; the launch traced here: 144 us
  starting transfers between devices  53.7 us (37%)
  waiting for transfers between devices  46 us (32%)
  local copies, waits for them, and re-layouts  15.7 us (11%)
  other arithmetic  10 us (7%)
  between operations  8.67 us (6%)
  Pallas kernels  5.19 us (4%)
  matrix products  4.31 us (3%)
    all_to_all x1, waiting for transfers between devices, body(): owned = lax.all_to_all(chip, PLANE, 0, 0)  23.8 us
    all_to_all x1, starting transfers between devices, body(): plane = lax.all_to_all(copies, PLANE, 0, 0)  21.1 us
    ppermute x4, waiting for transfers between devices, from_behind(): return lax.ppermute(value, axes, pairs)  12.9 us
    all_to_all x1, starting transfers between devices, body(): owned = lax.all_to_all(chip, PLANE, 0, 0)  11.9 us
    all_to_all x1, starting transfers between devices, body(): group = lax.all_to_all(group, DATA, 0, 0)  10.9 us
    ppermute x4, starting transfers between devices, from_behind(): return lax.ppermute(value, axes, pairs)  9.91 us
    all_to_all x1, waiting for transfers between devices, body(): group = lax.all_to_all(group, DATA, 0, 0)  9.29 us
    pallas_call x2, Pallas kernels, vmem_call(): pl.pallas_call(kernel, out_shape=shapes, in_specs=specs, out_specs=[pl.Bl...  5.19 us
  transfers between devices with their start and end apart: 7, of which 6 were waited for; matrix products, arithmetic and copies ran while one was open for 17% of the time, Pallas kernels for 0%

profile of v2, /device:TPU:16, one launch (start us, length us, event | category | flops | bytes accessed | tf_op | source)
XLA Modules:
  0.0 143.7 jit_solution(17028085346516366491)
XLA Ops:
  0.7 1.5 %copy.19 = bf16[144,6144]{1,0:T(8,128)(2,1)S(1)} copy(bf16[144,6144]{1,0:T(8,128)(2,1)} %param.6) | data formatting | bytes 3538944
  2.2 1.1 shard_map.93
  3.3 21.1 %all-to-all-start = ((bf16[32,40,384]{2,1,0:T(8,128)(2,1)}), bf16[32,40,384]{2,1,0:T(8,128)(2,1)S(1)}, u32[]{:S(2)}, u32[]{:S(2)}) async-start(bf16[32,40,384]{2,1,0:T(8,128)(2,1)} %shard_map.93), calls=%async_computation | async-start | bytes 1966080 | tf_op jit(solution)/shard_map/all_to_all | solution.py:136
  32.5 1.9 %concatenate.6 = bf16[37,6144]{1,0:T(8,128)(2,1)} pad(bf16[36,6144]{1,0:T(8,128)(2,1)} %get-tuple-element.17, bf16[]{:T(256)} %bitcast.2), padding=0_1x0_0 | pad | bytes 897026 | tf_op jit(solution)/shard_map/concatenate | solution.py:112
  34.3 3.6 %collective-permute-start = (bf16[37,6144]{1,0:T(8,128)(2,1)}, bf16[37,6144]{1,0:T(8,128)(2,1)}, u32[]{:S(2)}, u32[]{:S(2)}) collective-permute-start(bf16[37,6144]{1,0:T(8,128)(2,1)} %concatenate.6), channel_id=1, source_target_pairs={{0,64},{64,128},{128,192},{192,256},{256,320},{320,384},{384,448},... | collective-permute-start | bytes 1363976 | tf_op jit(solution)/shard_map/ppermute | solution.py:24
  39.4 2.2 %collective-permute-start.1 = (bf16[37,6144]{1,0:T(8,128)(2,1)}, bf16[37,6144]{1,0:T(8,128)(2,1)S(1)}, u32[]{:S(2)}, u32[]{:S(2)}) collective-permute-start(bf16[37,6144]{1,0:T(8,128)(2,1)} %concatenate.7), channel_id=1, source_target_pairs={{0,960},{64,0},{128,64},{192,128},{256,192},{320,256},{384,320},{4... | collective-permute-start | bytes 1363976 | tf_op jit(solution)/shard_map/ppermute | solution.py:24
  41.8 7.4 %collective-permute-done = bf16[37,6144]{1,0:T(8,128)(2,1)} collective-permute-done((bf16[37,6144]{1,0:T(8,128)(2,1)}, bf16[37,6144]{1,0:T(8,128)(2,1)}, u32[]{:S(2)}, u32[]{:S(2)}) %collective-permute-start) | collective-permute-done | bytes 454688 | tf_op jit(solution)/shard_map/ppermute | solution.py:24
  49.2 3.5 %dynamic_update_slice.6 = bf16[144,6144]{1,0:T(8,128)(2,1)S(1)} dynamic-update-slice(bf16[144,6144]{1,0:T(8,128)(2,1)S(1)} %copy.19, bf16[36,6144]{1,0:T(8,128)(2,1)} %bitcast.19, s32[]{:T(128)S(6)} %select_n.62, s32[]{:T(128)} %constant.41.clone.1) | dynamic-update-slice | bytes 884740 | tf_op jit(solution)/shard_map/dynamic_update_slice | solution.py:116
  52.7 1.2 collective-permute-done.1
  55.1 1.2 slice.31
  56.9 1.3 compare_select_fusion.1
  58.4 2.3 %dynamic_update_slice.7 = bf16[144,6144]{1,0:T(8,128)(2,1)S(1)} dynamic-update-slice(bf16[144,6144]{1,0:T(8,128)(2,1)S(1)} %dynamic_update_slice.6, bf16[36,6144]{1,0:T(8,128)(2,1)S(1)} %bitcast.23, s32[]{:T(128)S(6)} %select_n.60, s32[]{:T(128)} %constant.41.clone.1) | dynamic-update-slice | bytes 884740 | tf_op jit(solution)/shard_map/dynamic_update_slice | solution.py:117
  61.7 1.9 %collective-permute-start.2 = (bf16[32,40,384]{2,1,0:T(8,128)(2,1)S(1)}, bf16[32,40,384]{2,1,0:T(8,128)(2,1)S(1)}, u32[]{:S(2)}, u32[]{:S(2)}) collective-permute-start(bf16[32,40,384]{2,1,0:T(8,128)(2,1)S(1)} %all-to-all-done.own_ref), channel_id=1, source_target_pairs={{0,1},{1,0},{2,3},{3,2},{4,5},{5,4},{6,7},{7,6},{8,9},{9,8},{10,11... | collective-permute-start | bytes 2949128 | tf_op jit(solution)/shard_map/ppermute | solution.py:24
  64.3 1.9 %collective-permute-done.2.partner_ref = bf16[32,40,384]{2,1,0:T(8,128)(2,1)S(1)} collective-permute-done((bf16[32,40,384]{2,1,0:T(8,128)(2,1)S(1)}, bf16[32,40,384]{2,1,0:T(8,128)(2,1)S(1)}, u32[]{:S(2)}, u32[]{:S(2)}) %collective-permute-start.2) | collective-permute-done | bytes 983072 | tf_op jit(solution)/shard_map/ppermute | solution.py:24
  66.2 4.1 %shard_map.94 = (bf16[144,150]{1,0:T(8,128)(2,1)}, bf16[144,192]{1,0:T(8,128)(2,1)S(1)}, bf16[192,6144]{1,0:T(8,128)(2,1)S(1)}, bf16[32,40,384]{2,1,0:T(8,128)(2,1)S(1)}, bf16[32,40,384]{2,1,0:T(8,128)(2,1)S(1)}) custom-call(s32[1]{0:T(128)} %bitcast.core_ref, bf16[144,6144]{1,0:T(8,128)(2,1)S(1)} %fusion.4.act_ref, ...), custom_call_target="tpu_custom_call" | custom-call | flops 679477248 | bytes 12582912 | tf_op jit(solution)/shard_map/pallas_call | solution.py:32
  70.9 2.2 %collective-permute-start.3 = (bf16[32,40,384]{2,1,0:T(8,128)(2,1)S(1)}, bf16[32,40,384]{2,1,0:T(8,128)(2,1)S(1)}, u32[]{:S(2)}, u32[]{:S(2)}) collective-permute-start(bf16[32,40,384]{2,1,0:T(8,128)(2,1)S(1)} %get-tuple-element.13), channel_id=1, source_target_pairs={{0,1},{1,0},{2,3},{3,2},{4,5},{5,4},{6,7},{7,6},{8,9},{9,8},{10,11... | collective-permute-start | bytes 2949128 | tf_op jit(solution)/shard_map/ppermute | solution.py:24
  73.1 2.4 %collective-permute-done.3 = bf16[32,40,384]{2,1,0:T(8,128)(2,1)S(1)} collective-permute-done((bf16[32,40,384]{2,1,0:T(8,128)(2,1)S(1)}, bf16[32,40,384]{2,1,0:T(8,128)(2,1)S(1)}, u32[]{:S(2)}, u32[]{:S(2)}) %collective-permute-start.3) | collective-permute-done | bytes 983072 | tf_op jit(solution)/shard_map/ppermute | solution.py:24
  75.5 1.2 add_convert_fusion
  76.7 11.9 %all-to-all-start.1 = ((bf16[32,40,384]{2,1,0:T(8,128)(2,1)}), bf16[32,40,384]{2,1,0:T(8,128)(2,1)S(1)}, u32[]{:S(2)}, u32[]{:S(2)}) async-start(bf16[32,40,384]{2,1,0:T(8,128)(2,1)} %add_convert_fusion), calls=%async_computation.1 | async-start | bytes 1966080 | tf_op jit(solution)/shard_map/all_to_all | solution.py:171
  88.6 4.3 %fusion.13 = (f32[144]{0:T(256)S(1)}, f32[144]{0:T(256)S(1)}, f32[144,6144]{1,0:T(8,128)}) fusion(f32[144]{0:T(256)S(1)} %add_rsqrt_fusion, f32[144]{0:T(256)S(1)} %broadcast_multiply_fusion.2, bf16[144,6144]{1,0:T(8,128)(2,1)} %copy-done.4, bf16[144,192]{1,0:T(8,128)(2,1)S(1)} %copy-done.2, bf16[192,6144]{1,0:T(8,128)(2,1)S(1)} %get-tuple-element.11), kind=kOutput, calls=%fused_computation.36 | convolution fusion | flops 345046784 | bytes 7725312 | tf_op jit(solution)/shard_map/dot_general | solution.py:166
  92.9 23.8 %all-to-all-done.1 = bf16[32,40,384]{2,1,0:T(8,128)(2,1)S(1)} async-done(((bf16[32,40,384]{2,1,0:T(8,128)(2,1)}), bf16[32,40,384]{2,1,0:T(8,128)(2,1)S(1)}, u32[]{:S(2)}, u32[]{:S(2)}) %all-to-all-start.1) | async-done | bytes 983072 | tf_op jit(solution)/shard_map/all_to_all | solution.py:171
  117.7 10.9 %all-to-all-start.2 = ((bf16[16,40,384]{2,1,0:T(8,128)(2,1)}), bf16[16,40,384]{2,1,0:T(8,128)(2,1)S(1)}, u32[]{:S(2)}, u32[]{:S(2)}) async-start(bf16[16,40,384]{2,1,0:T(8,128)(2,1)} %broadcast_in_dim.51), calls=%async_computation.2 | async-start | bytes 983040 | tf_op jit(solution)/shard_map/all_to_all | solution.py:174
  128.6 4.5 %fusion.8 = bf16[144,6144]{1,0:T(8,128)(2,1)} fusion(bf16[144,6144]{1,0:T(8,128)(2,1)S(1)} %copy-done.5, f32[144,6144]{1,0:T(8,128)} %get-tuple-element.24, f32[144]{0:T(256)S(1)} %get-tuple-element.25, f32[144]{0:T(256)S(1)} %get-tuple-element.26, f32[144]{0:T(256)S(1)} %add_rsqrt_fusion, f32[144]{0:T(256)S(1)} %broadcast_multiply_fusion.2), kind=kLoop, calls=%fused_computation.10 | loop fusion | flops 7077888 | bytes 7080192 | tf_op jit(solution)/shard_map/convert_element_type | solution.py:169
  133.0 9.3 %all-to-all-done.2 = bf16[16,40,384]{2,1,0:T(8,128)(2,1)S(1)} async-done(((bf16[16,40,384]{2,1,0:T(8,128)(2,1)}), bf16[16,40,384]{2,1,0:T(8,128)(2,1)S(1)}, u32[]{:S(2)}, u32[]{:S(2)}) %all-to-all-start.2) | async-done | bytes 491552 | tf_op jit(solution)/shard_map/all_to_all | solution.py:174
  (42 shorter events, 8.4 us)
Async XLA Ops:
  0.6 1.5 %copy-start = (bf16[96,150]{0,1:T(8,128)(2,1)S(1)}, bf16[96,150]{0,1:T(8,128)(2,1)}, u32[]{:S(2)}) copy-start(bf16[96,150]{0,1:T(8,128)(2,1)} %param.8) | copy-start | bytes 86404
  0.6 1.5 %copy-start.3 = (bf16[96]{0:T(256)(128)(2,1)S(1)}, bf16[96]{0:T(256)(128)(2,1)}, u32[]{:S(2)}) copy-start(bf16[96]{0:T(256)(128)(2,1)} %param.9) | copy-start | bytes 580
  0.7 30.5 %copy-start.6 = (s32[4]{0:T(128)S(1)}, s32[4]{0:T(128)}, u32[]{:S(2)}) copy-start(s32[4]{0:T(128)} %param.10) | copy-start | bytes 52
  0.7 23.7 %copy-start.7 = (s32[1,2]{1,0:T(1,128)S(1)}, s32[1,2]{1,0:T(1,128)}, u32[]{:S(2)}) copy-start(s32[1,2]{1,0:T(1,128)} %param.11) | copy-start | bytes 28
  2.2 39.5 %copy-start.8 = (s32[144]{0:T(256)S(1)}, s32[144]{0:T(256)}, u32[]{:S(2)}) copy-start(s32[144]{0:T(256)} %param.7) | copy-start | bytes 1732
  3.3 58.4 %all-to-all-start = ((bf16[32,40,384]{2,1,0:T(8,128)(2,1)}), bf16[32,40,384]{2,1,0:T(8,128)(2,1)S(1)}, u32[]{:S(2)}, u32[]{:S(2)}) async-start(bf16[32,40,384]{2,1,0:T(8,128)(2,1)} %shard_map.93), calls=%async_computation | async-start | bytes 1966080 | tf_op jit(solution)/shard_map/all_to_all | solution.py:136
  34.3 14.9 %collective-permute-start = (bf16[37,6144]{1,0:T(8,128)(2,1)}, bf16[37,6144]{1,0:T(8,128)(2,1)}, u32[]{:S(2)}, u32[]{:S(2)}) collective-permute-start(bf16[37,6144]{1,0:T(8,128)(2,1)} %concatenate.6), channel_id=1, source_target_pairs={{0,64},{64,128},{128,192},{192,256},{256,320},{320,384},{384,448},... | collective-permute-start | bytes 1363976 | tf_op jit(solution)/shard_map/ppermute | solution.py:24
  39.4 14.5 %collective-permute-start.1 = (bf16[37,6144]{1,0:T(8,128)(2,1)}, bf16[37,6144]{1,0:T(8,128)(2,1)S(1)}, u32[]{:S(2)}, u32[]{:S(2)}) collective-permute-start(bf16[37,6144]{1,0:T(8,128)(2,1)} %concatenate.7), channel_id=1, source_target_pairs={{0,960},{64,0},{128,64},{192,128},{256,192},{320,256},{384,320},{4... | collective-permute-start | bytes 1363976 | tf_op jit(solution)/shard_map/ppermute | solution.py:24
  60.7 3.6 %copy-start.4 = (bf16[144,6144]{1,0:T(8,128)(2,1)}, bf16[144,6144]{1,0:T(8,128)(2,1)S(1)}, u32[]{:S(2)}) copy-start(bf16[144,6144]{1,0:T(8,128)(2,1)S(1)} %dynamic_update_slice.7) | copy-start | bytes 5308420
  61.7 4.5 %collective-permute-start.2 = (bf16[32,40,384]{2,1,0:T(8,128)(2,1)S(1)}, bf16[32,40,384]{2,1,0:T(8,128)(2,1)S(1)}, u32[]{:S(2)}, u32[]{:S(2)}) collective-permute-start(bf16[32,40,384]{2,1,0:T(8,128)(2,1)S(1)} %all-to-all-done.own_ref), channel_id=1, source_target_pairs={{0,1},{1,0},{2,3},{3,2},{4,5},{5,4},{6,7},{7,6},{8,9},{9,8},{10,11... | collective-permute-start | bytes 2949128 | tf_op jit(solution)/shard_map/ppermute | solution.py:24
  70.3 0.6 copy-start.1
  70.9 17.7 %copy-start.2 = (bf16[144,192]{1,0:T(8,128)(2,1)S(1)}, bf16[144,192]{1,0:T(8,128)(2,1)}, u32[]{:S(2)}) copy-start(bf16[144,192]{1,0:T(8,128)(2,1)} %copy-done.1) | copy-start | bytes 165892
  70.9 4.6 %collective-permute-start.3 = (bf16[32,40,384]{2,1,0:T(8,128)(2,1)S(1)}, bf16[32,40,384]{2,1,0:T(8,128)(2,1)S(1)}, u32[]{:S(2)}, u32[]{:S(2)}) collective-permute-start(bf16[32,40,384]{2,1,0:T(8,128)(2,1)S(1)} %get-tuple-element.13), channel_id=1, source_target_pairs={{0,1},{1,0},{2,3},{3,2},{4,5},{5,4},{6,7},{7,6},{8,9},{9,8},{10,11... | collective-permute-start | bytes 2949128 | tf_op jit(solution)/shard_map/ppermute | solution.py:24
  76.7 40.0 %all-to-all-start.1 = ((bf16[32,40,384]{2,1,0:T(8,128)(2,1)}), bf16[32,40,384]{2,1,0:T(8,128)(2,1)S(1)}, u32[]{:S(2)}, u32[]{:S(2)}) async-start(bf16[32,40,384]{2,1,0:T(8,128)(2,1)} %add_convert_fusion), calls=%async_computation.1 | async-start | bytes 1966080 | tf_op jit(solution)/shard_map/all_to_all | solution.py:171
  92.9 35.7 %copy-start.5 = (bf16[144,6144]{1,0:T(8,128)(2,1)S(1)}, bf16[144,6144]{1,0:T(8,128)(2,1)}, u32[]{:S(2)}) copy-start(bf16[144,6144]{1,0:T(8,128)(2,1)} %copy-done.4) | copy-start | bytes 5308420
  117.7 24.6 %all-to-all-start.2 = ((bf16[16,40,384]{2,1,0:T(8,128)(2,1)}), bf16[16,40,384]{2,1,0:T(8,128)(2,1)S(1)}, u32[]{:S(2)}, u32[]{:S(2)}) async-start(bf16[16,40,384]{2,1,0:T(8,128)(2,1)} %broadcast_in_dim.51), calls=%async_computation.2 | async-start | bytes 983040 | tf_op jit(solution)/shard_map/all_to_all | solution.py:174

commit v3 on v2

--- a/solution.py
+++ b/solution.py
@@ -24,7 +24,7 @@
     return lax.ppermute(value, axes, pairs)
 
 
-def vmem_call(kernel, shapes, cost, *operands, scalars=0):
+def vmem_call(kernel, shapes, cost, *operands, scalars=0, scratch=()):
     specs = [
         pl.BlockSpec(memory_space=pltpu.SMEM if place < scalars else pltpu.VMEM)
         for place in range(len(operands))
@@ -34,6 +34,7 @@
         out_shape=shapes,
         in_specs=specs,
         out_specs=[pl.BlockSpec(memory_space=pltpu.VMEM)] * len(shapes),
+        scratch_shapes=list(scratch),
         compiler_params=pltpu.CompilerParams(vmem_limit_bytes=32 * 1024 * 1024),
         cost_estimate=pl.CostEstimate(flops=cost[0], bytes_accessed=cost[1], transcendentals=0),
     )(*operands)
@@ -100,30 +101,56 @@
             send_ref[2 * q + half] = jnp.where(first, odd, even)
 
 
-def move(patches, counts, plan):
-    total_rows, width = patches.shape
-    slot_count = counts.shape[0]
-    patch = total_rows // slot_count
-    up, down = plan[0, 0], plan[0, 1]
-
-    def parcel(slot):
-        image = lax.dynamic_slice(patches, (slot * patch, 0), (patch, width))
-        count = lax.dynamic_slice_in_dim(counts, slot, 1).astype(jnp.bfloat16)
-        return jnp.concatenate([image, jnp.broadcast_to(count[:, None], (1, width))])
-
-    arrive_low = from_behind(parcel(up), DATA, 1)
-    arrive_up = from_behind(parcel(down), DATA, -1)
-    rows = lax.dynamic_update_slice(patches, arrive_low[:patch], (down * patch, 0))
-    rows = lax.dynamic_update_slice(rows, arrive_up[:patch], (up * patch, 0))
-    slot_ids = jnp.arange(slot_count, dtype=jnp.int32)
-    live = jnp.where(
-        slot_ids == up,
-        arrive_up[patch, 0].astype(jnp.int32),
-        jnp.where(slot_ids == down, arrive_low[patch, 0].astype(jnp.int32), counts),
-    )
-    places = jnp.arange(patch, dtype=jnp.int32)
-    mask = (places[None, :] < live[:, None]).astype(jnp.float32).reshape(-1, 1)
-    return rows, mask
+def parcel_kernel(plan_ref, counts_ref, patches_ref, up_ref, down_ref):
+    slots = counts_ref.shape[0]
+    patch = patches_ref.shape[0] // slots
+    for way, out_ref in ((0, up_ref), (1, down_ref)):
+        for slot in range(slots):
+
+            @pl.when(plan_ref[0, way] == slot)
+            def _(slot=slot, out_ref=out_ref):
+                begin = slot * patch // 16 * 16
+                end = min(-(-(slot + 1) * patch // 16) * 16, patches_ref.shape[0])
+                window = patches_ref[begin:end].astype(jnp.float32)
+                image = window[slot * patch - begin : (slot + 1) * patch - begin]
+                count = jnp.full((1, image.shape[1]), counts_ref[slot].astype(jnp.float32))
+                out_ref[...] = jnp.concatenate([image, count], axis=0).astype(jnp.bfloat16)
+
+
+def norm_kernel(
+    plan_ref, counts_ref, patches_ref, low_ref, high_ref,
+    act_ref, inverse_ref, mask_ref, rows_ref,
+):
+    slots = counts_ref.shape[0]
+    total_rows, width = patches_ref.shape
+    patch = total_rows // slots
+    up, down = plan_ref[0, 0], plan_ref[0, 1]
+    rows_ref[...] = patches_ref[...].astype(jnp.float32)
+    for slot in range(slots):
+
+        @pl.when(up == slot)
+        def _(slot=slot):
+            rows_ref[slot * patch : (slot + 1) * patch] = high_ref[:patch].astype(jnp.float32)
+
+        @pl.when(down == slot)
+        def _(slot=slot):
+            rows_ref[slot * patch : (slot + 1) * patch] = low_ref[:patch].astype(jnp.float32)
+
+    high_live = high_ref[patch : patch + 1, :1].astype(jnp.float32)
+    low_live = low_ref[patch : patch + 1, :1].astype(jnp.float32)
+    places = lax.broadcasted_iota(jnp.int32, (patch, 1), 0).astype(jnp.float32)
+    masks = []
+    for slot in range(slots):
+        own_live = jnp.full((1, 1), counts_ref[slot].astype(jnp.float32))
+        live = jnp.where(up == slot, high_live, jnp.where(down == slot, low_live, own_live))
+        masks.append(jnp.where(places < live, 1.0, 0.0))
+    mask_ref[...] = jnp.concatenate(masks, axis=0)
+    for begin in range(0, total_rows, 16):
+        rows = rows_ref[begin : begin + 16]
+        centred = rows - jnp.mean(rows, axis=1, keepdims=True)
+        inverse = lax.rsqrt(jnp.mean(centred * centred, axis=1, keepdims=True) + 1e-06)
+        act_ref[begin : begin + 16] = (centred * inverse).astype(jnp.bfloat16)
+        inverse_ref[begin : begin + 16] = inverse
 
 
 def body(patches, labels, weight, gain, counts, plan):
@@ -135,13 +162,21 @@
     (copies,) = vmem_call(prepare_kernel, [wire], (0, 2**20), weight.T, gain[None, :])
     plane = lax.all_to_all(copies, PLANE, 0, 0)
 
-    rows, mask = move(patches, counts, plan)
-    rows32 = rows.astype(jnp.float32)
-    average = jnp.mean(rows32, axis=1, keepdims=True)
-    centred = rows32 - average
-    inverse = lax.rsqrt(jnp.mean(centred * centred, axis=1, keepdims=True) + 1e-06)
-    normed = centred * inverse
-    act = normed.astype(jnp.bfloat16)
+    image = jax.ShapeDtypeStruct((total_rows // counts.shape[0] + 1, width), jnp.bfloat16)
+    column = jax.ShapeDtypeStruct((total_rows, 1), jnp.float32)
+    up, down = vmem_call(
+        parcel_kernel, [image, image], (0, 3 * 2**20), plan, counts, patches, scalars=2
+    )
+    arrive_low = from_behind(up, DATA, 1)
+    arrive_up = from_behind(down, DATA, -1)
+    act, inverse, mask = vmem_call(
+        norm_kernel,
+        [jax.ShapeDtypeStruct((total_rows, width), jnp.bfloat16), column, column],
+        (10 * total_rows * width, 5 * 2**20),
+        plan, counts, patches, arrive_low, arrive_up,
+        scalars=2,
+        scratch=[pltpu.VMEM((total_rows, width), jnp.float32)],
+    )
 
     partner = from_behind(plane, "core", 1)
     slots = jnp.arange(INNER, dtype=jnp.int32)
@@ -165,6 +200,7 @@
 
     dnorm = jnp.dot(dpre, full, preferred_element_type=jnp.float32)
     first = jnp.mean(dnorm, axis=1, keepdims=True)
+    normed = act.astype(jnp.float32)
     second = jnp.mean(dnorm * normed, axis=1, keepdims=True)
     input_grad = (inverse * (dnorm - first - normed * second)).astype(jnp.bfloat16)
 

time: 145 us -> 154 us (1.062)
  the two profiles are of different devices: /device:TPU:16 before, /device:TPU:20 now
where the time goes in v3:
time: 154 us
  blocking collectives  49 us (32%)
  waiting for transfers between devices  46.6 us (30%)
  starting transfers between devices  25.8 us (17%)
  local copies, waits for them, and re-layouts  11.1 us (7%)
  Pallas kernels  9.29 us (6%)
  other arithmetic  6.81 us (4%)
  matrix products  4.2 us (3%)
    all_to_all x1, blocking collectives, body(): plane = lax.all_to_all(copies, PLANE, 0, 0)  49 us
    all_to_all x1, waiting for transfers between devices, body(): owned = lax.all_to_all(chip, PLANE, 0, 0)  23.5 us
    ppermute x4, waiting for transfers between devices, from_behind(): return lax.ppermute(value, axes, pairs)  13.9 us
    ppermute x4, starting transfers between devices, from_behind(): return lax.ppermute(value, axes, pairs)  9.65 us
    all_to_all x1, starting transfers between devices, body(): group = lax.all_to_all(group, DATA, 0, 0)  9.52 us
    unnamed x36, local copies, waits for them, and re-layouts  9.44 us
    pallas_call x4, Pallas kernels, vmem_call(): pl.pallas_call(kernel, out_shape=shapes, in_specs=specs, out_specs=[pl.Bl...  9.29 us
    all_to_all x1, waiting for transfers between devices, body(): group = lax.all_to_all(group, DATA, 0, 0)  9.18 us
  transfers between devices with their start and end apart: 6, of which 5 were waited for; matrix products, arithmetic and copies ran while one was open for 6% of the time, Pallas kernels for 2%

profile of v3, /device:TPU:20, one launch (start us, length us, event | category | flops | bytes accessed | tf_op | source)
XLA Modules:
  0.0 153.6 jit_solution(10469566696768322759)
XLA Ops:
  0.7 0.9 copy-done.7
  2.4 49.0 %all_to_all.15.own_ref = bf16[32,40,384]{2,1,0:T(8,128)(2,1)} all-to-all(bf16[32,40,384]{2,1,0:T(8,128)(2,1)S(1)} %shard_map.95), channel_id=1, replica_groups=mesh['z_lo'=2,'y'=8,'x'=8,'z_hi'=4,'core'=2] {'x','z_hi'}, dimensions={0} | all-to-all | bytes 1966080 | tf_op jit(solution)/shard_map/all_to_all | solution.py:163
  51.3 1.9 %collective-permute-start.2 = (bf16[32,40,384]{2,1,0:T(8,128)(2,1)}, bf16[32,40,384]{2,1,0:T(8,128)(2,1)}, u32[]{:S(2)}, u32[]{:S(2)}) collective-permute-start(bf16[32,40,384]{2,1,0:T(8,128)(2,1)} %all_to_all.15.own_ref), channel_id=1, source_target_pairs={{0,1},{1,0},{2,3},{3,2},{4,5},{5,4},{6,7},{7,6},{8,9},{9,8},{10,11... | collective-permute-start | bytes 2949128 | tf_op jit(solution)/shard_map/ppermute | solution.py:24
  54.6 1.6 %shard_map.93 = (bf16[37,6144]{1,0:T(8,128)(2,1)}, bf16[37,6144]{1,0:T(8,128)(2,1)S(1)}) custom-call(s32[1,2]{1,0:T(1,128)S(1)} %copy-done.11, s32[4]{0:T(128)S(1)} %copy-done.13, bf16[144,6144]{1,0:T(8,128)(2,1)S(1)} %copy-done), custom_call_target="tpu_custom_call" | custom-call | bytes 3145728 | tf_op jit(solution)/shard_map/pallas_call | solution.py:32
  56.2 3.6 %collective-permute-start = (bf16[37,6144]{1,0:T(8,128)(2,1)}, bf16[37,6144]{1,0:T(8,128)(2,1)S(1)}, u32[]{:S(2)}, u32[]{:S(2)}) collective-permute-start(bf16[37,6144]{1,0:T(8,128)(2,1)} %get-tuple-element.14), channel_id=1, source_target_pairs={{0,64},{64,128},{128,192},{192,256},{256,320},{320,384},{384,448},... | collective-permute-start | bytes 1363976 | tf_op jit(solution)/shard_map/ppermute | solution.py:24
  59.8 2.2 %collective-permute-start.1 = (bf16[37,6144]{1,0:T(8,128)(2,1)S(1)}, bf16[37,6144]{1,0:T(8,128)(2,1)S(1)}, u32[]{:S(2)}, u32[]{:S(2)}) collective-permute-start(bf16[37,6144]{1,0:T(8,128)(2,1)S(1)} %get-tuple-element.15), channel_id=1, source_target_pairs={{0,960},{64,0},{128,64},{192,128},{256,192},{320,256},{384,320},{4... | collective-permute-start | bytes 1363976 | tf_op jit(solution)/shard_map/ppermute | solution.py:24
  62.8 8.9 %collective-permute-done.low_ref = bf16[37,6144]{1,0:T(8,128)(2,1)S(1)} collective-permute-done((bf16[37,6144]{1,0:T(8,128)(2,1)}, bf16[37,6144]{1,0:T(8,128)(2,1)S(1)}, u32[]{:S(2)}, u32[]{:S(2)}) %collective-permute-start) | collective-permute-done | bytes 454688 | tf_op jit(solution)/shard_map/ppermute | solution.py:24
  72.5 2.4 %collective-permute-done.1.high_ref = bf16[37,6144]{1,0:T(8,128)(2,1)S(1)} collective-permute-done((bf16[37,6144]{1,0:T(8,128)(2,1)S(1)}, bf16[37,6144]{1,0:T(8,128)(2,1)S(1)}, u32[]{:S(2)}, u32[]{:S(2)}) %collective-permute-start.1) | collective-permute-done | bytes 454688 | tf_op jit(solution)/shard_map/ppermute | solution.py:24
  75.8 1.0 copy-done.3
  76.8 1.0 copy-done.5
  77.8 1.9 %shard_map.94 = (bf16[144,6144]{1,0:T(8,128)(2,1)S(1)}, f32[144,1]{1,0:T(8,128)S(1)}, f32[144,1]{1,0:T(8,128)S(1)}) custom-call(s32[1,2]{1,0:T(1,128)S(1)} %copy-done.12, s32[4]{0:T(128)S(1)} %copy-done.14, bf16[144,6144]{1,0:T(8,128)(2,1)S(1)} %copy-done, bf16[37,6144]{1,0:T(8,128)(2,1)S(1)} %copy-done.3, bf16[37,6144]{1,0:T(8,128)(2,1)S(1)} %copy-done.5), custom_call_target="tpu_custom_call" | custom-call | flops 8847360 | bytes 5242880 | tf_op jit(solution)/shard_map/pallas_call | solution.py:32
  80.4 0.9 copy-done.6
  81.3 5.6 %shard_map.96 = (bf16[144,150]{1,0:T(8,128)(2,1)}, bf16[144,192]{1,0:T(8,128)(2,1)S(1)}, bf16[192,6144]{1,0:T(8,128)(2,1)S(1)}, bf16[32,40,384]{2,1,0:T(8,128)(2,1)S(1)}, bf16[32,40,384]{2,1,0:T(8,128)(2,1)S(1)}) custom-call(s32[1]{0:T(128)} %bitcast.core_ref, bf16[144,6144]{1,0:T(8,128)(2,1)S(1)} %get-tuple-element.16.act_ref, ...), custom_call_target="tpu_custom_call" | custom-call | flops 679477248 | bytes 12582912 | tf_op jit(solution)/shard_map/pallas_call | solution.py:32
  86.9 1.4 copy-done.1
  88.3 1.9 %collective-permute-start.3 = (bf16[32,40,384]{2,1,0:T(8,128)(2,1)S(1)}, bf16[32,40,384]{2,1,0:T(8,128)(2,1)S(1)}, u32[]{:S(2)}, u32[]{:S(2)}) collective-permute-start(bf16[32,40,384]{2,1,0:T(8,128)(2,1)S(1)} %get-tuple-element.23), channel_id=1, source_target_pairs={{0,1},{1,0},{2,3},{3,2},{4,5},{5,4},{6,7},{7,6},{8,9},{9,8},{10,11... | collective-permute-start | bytes 2949128 | tf_op jit(solution)/shard_map/ppermute | solution.py:24
  90.2 2.5 %collective-permute-done.3 = bf16[32,40,384]{2,1,0:T(8,128)(2,1)S(1)} collective-permute-done((bf16[32,40,384]{2,1,0:T(8,128)(2,1)S(1)}, bf16[32,40,384]{2,1,0:T(8,128)(2,1)S(1)}, u32[]{:S(2)}, u32[]{:S(2)}) %collective-permute-start.3) | collective-permute-done | bytes 983072 | tf_op jit(solution)/shard_map/ppermute | solution.py:24
  92.7 1.2 add_convert_fusion
  94.0 6.6 %all-to-all-start.1 = ((bf16[32,40,384]{2,1,0:T(8,128)(2,1)}), bf16[32,40,384]{2,1,0:T(8,128)(2,1)S(1)}, u32[]{:S(2)}, u32[]{:S(2)}) async-start(bf16[32,40,384]{2,1,0:T(8,128)(2,1)} %add_convert_fusion), calls=%async_computation.1 | async-start | bytes 1966080 | tf_op jit(solution)/shard_map/all_to_all | solution.py:207
  100.7 4.2 %fusion.6 = (f32[144]{0:T(256)S(1)}, f32[144]{0:T(256)S(1)}, f32[144,6144]{1,0:T(8,128)}) fusion(bf16[144,6144]{1,0:T(8,128)(2,1)S(1)} %get-tuple-element.16.act_ref, bf16[144,192]{1,0:T(8,128)(2,1)S(1)} %get-tuple-element.20, bf16[192,6144]{1,0:T(8,128)(2,1)} %copy-done.1), kind=kOutput, calls=%fused_computation.22 | convolution fusion | flops 343277312 | bytes 7724160 | tf_op jit(solution)/shard_map/dot_general | solution.py:201
  104.9 23.5 %all-to-all-done.1 = bf16[32,40,384]{2,1,0:T(8,128)(2,1)S(1)} async-done(((bf16[32,40,384]{2,1,0:T(8,128)(2,1)}), bf16[32,40,384]{2,1,0:T(8,128)(2,1)S(1)}, u32[]{:S(2)}, u32[]{:S(2)}) %all-to-all-start.1) | async-done | bytes 983072 | tf_op jit(solution)/shard_map/all_to_all | solution.py:207
  128.6 0.8 broadcast_in_dim.24
  129.4 9.5 %all-to-all-start.2 = ((bf16[16,40,384]{2,1,0:T(8,128)(2,1)}), bf16[16,40,384]{2,1,0:T(8,128)(2,1)S(1)}, u32[]{:S(2)}, u32[]{:S(2)}) async-start(bf16[16,40,384]{2,1,0:T(8,128)(2,1)} %broadcast_in_dim.24), calls=%async_computation.2 | async-start | bytes 983040 | tf_op jit(solution)/shard_map/all_to_all | solution.py:210
  138.9 4.1 %fusion.3 = bf16[144,6144]{1,0:T(8,128)(2,1)} fusion(bf16[144,6144]{1,0:T(8,128)(2,1)S(1)} %get-tuple-element.16.act_ref, f32[144,6144]{1,0:T(8,128)} %get-tuple-element.28, f32[144]{0:T(256)S(1)} %get-tuple-element.29, f32[144]{0:T(256)S(1)} %get-tuple-element.30, f32[144]{0:T(256)S(1)} %reduce.1), kind=kLoop, calls=%fused_computation.5 | loop fusion | flops 5308416 | bytes 7079616 | tf_op jit(solution)/shard_map/convert_element_type | solution.py:205
  143.0 9.2 %all-to-all-done.2 = bf16[16,40,384]{2,1,0:T(8,128)(2,1)S(1)} async-done(((bf16[16,40,384]{2,1,0:T(8,128)(2,1)}), bf16[16,40,384]{2,1,0:T(8,128)(2,1)S(1)}, u32[]{:S(2)}, u32[]{:S(2)}) %all-to-all-start.2) | async-done | bytes 491552 | tf_op jit(solution)/shard_map/all_to_all | solution.py:210
  (44 shorter events, 6.7 us)
Async XLA Ops:
  0.6 52.6 %copy-start = (bf16[144,6144]{1,0:T(8,128)(2,1)S(1)}, bf16[144,6144]{1,0:T(8,128)(2,1)}, u32[]{:S(2)}) copy-start(bf16[144,6144]{1,0:T(8,128)(2,1)} %patches_ref.3) | copy-start | bytes 5308420
  0.6 0.9 copy-start.7
  1.5 0.7 copy-start.15
  2.2 59.8 %copy-start.17 = (s32[144]{0:T(256)S(1)}, s32[144]{0:T(256)}, u32[]{:S(2)}) copy-start(s32[144]{0:T(256)} %param.7) | copy-start | bytes 1732
  2.2 73.5 %copy-start.12 = (s32[1,2]{1,0:T(1,128)S(1)}, s32[1,2]{1,0:T(1,128)}, u32[]{:S(2)}) copy-start(s32[1,2]{1,0:T(1,128)} %plan_ref.3) | copy-start | bytes 28
  2.2 73.5 %copy-start.14 = (s32[4]{0:T(128)S(1)}, s32[4]{0:T(128)}, u32[]{:S(2)}) copy-start(s32[4]{0:T(128)} %counts_ref.3) | copy-start | bytes 52
  51.3 29.1 %collective-permute-start.2 = (bf16[32,40,384]{2,1,0:T(8,128)(2,1)}, bf16[32,40,384]{2,1,0:T(8,128)(2,1)}, u32[]{:S(2)}, u32[]{:S(2)}) collective-permute-start(bf16[32,40,384]{2,1,0:T(8,128)(2,1)} %all_to_all.15.own_ref), channel_id=1, source_target_pairs={{0,1},{1,0},{2,3},{3,2},{4,5},{5,4},{6,7},{7,6},{8,9},{9,8},{10,11... | collective-permute-start | bytes 2949128 | tf_op jit(solution)/shard_map/ppermute | solution.py:24
  53.3 0.7 copy-start.11
  53.9 0.7 copy-start.13
  56.2 15.6 %collective-permute-start = (bf16[37,6144]{1,0:T(8,128)(2,1)}, bf16[37,6144]{1,0:T(8,128)(2,1)S(1)}, u32[]{:S(2)}, u32[]{:S(2)}) collective-permute-start(bf16[37,6144]{1,0:T(8,128)(2,1)} %get-tuple-element.14), channel_id=1, source_target_pairs={{0,64},{64,128},{128,192},{192,256},{256,320},{320,384},{384,448},... | collective-permute-start | bytes 1363976 | tf_op jit(solution)/shard_map/ppermute | solution.py:24
  59.8 15.2 %collective-permute-start.1 = (bf16[37,6144]{1,0:T(8,128)(2,1)S(1)}, bf16[37,6144]{1,0:T(8,128)(2,1)S(1)}, u32[]{:S(2)}, u32[]{:S(2)}) collective-permute-start(bf16[37,6144]{1,0:T(8,128)(2,1)S(1)} %get-tuple-element.15), channel_id=1, source_target_pairs={{0,960},{64,0},{128,64},{192,128},{256,192},{320,256},{384,320},{4... | collective-permute-start | bytes 1363976 | tf_op jit(solution)/shard_map/ppermute | solution.py:24
  71.8 0.8 copy-start.2
  75.0 0.8 copy-start.4
  75.8 1.0 copy-start.3
  76.8 1.0 copy-start.5
  79.8 0.6 copy-start.9
  80.4 0.9 copy-start.6
  81.3 19.3 %copy-start.16 = (bf16[96]{0:T(256)(128)(2,1)S(1)}, bf16[96]{0:T(256)(128)(2,1)}, u32[]{:S(2)}) copy-start(bf16[96]{0:T(256)(128)(2,1)} %param.9) | copy-start | bytes 580
  81.3 19.3 %copy-start.10 = (f32[144,1]{1,0:T(8,128)S(1)}, f32[144,1]{1,0:T(8,128)}, u32[]{:S(2)}) copy-start(f32[144,1]{1,0:T(8,128)} %copy-done.9) | copy-start | bytes 1732
  86.9 1.4 copy-start.1
  88.3 4.4 %collective-permute-start.3 = (bf16[32,40,384]{2,1,0:T(8,128)(2,1)S(1)}, bf16[32,40,384]{2,1,0:T(8,128)(2,1)S(1)}, u32[]{:S(2)}, u32[]{:S(2)}) collective-permute-start(bf16[32,40,384]{2,1,0:T(8,128)(2,1)S(1)} %get-tuple-element.23), channel_id=1, source_target_pairs={{0,1},{1,0},{2,3},{3,2},{4,5},{5,4},{6,7},{7,6},{8,9},{9,8},{10,11... | collective-permute-start | bytes 2949128 | tf_op jit(solution)/shard_map/ppermute | solution.py:24
  94.0 34.5 %all-to-all-start.1 = ((bf16[32,40,384]{2,1,0:T(8,128)(2,1)}), bf16[32,40,384]{2,1,0:T(8,128)(2,1)S(1)}, u32[]{:S(2)}, u32[]{:S(2)}) async-start(bf16[32,40,384]{2,1,0:T(8,128)(2,1)} %add_convert_fusion), calls=%async_computation.1 | async-start | bytes 1966080 | tf_op jit(solution)/shard_map/all_to_all | solution.py:207
  129.4 22.8 %all-to-all-start.2 = ((bf16[16,40,384]{2,1,0:T(8,128)(2,1)}), bf16[16,40,384]{2,1,0:T(8,128)(2,1)S(1)}, u32[]{:S(2)}, u32[]{:S(2)}) async-start(bf16[16,40,384]{2,1,0:T(8,128)(2,1)} %broadcast_in_dim.24), calls=%async_computation.2 | async-start | bytes 983040 | tf_op jit(solution)/shard_map/all_to_all | solution.py:210
  138.9 13.5 %copy-start.8 = (bf16[96,150]{0,1:T(8,128)(2,1)S(1)}, bf16[96,150]{0,1:T(8,128)(2,1)}, u32[]{:S(2)}) copy-start(bf16[96,150]{0,1:T(8,128)(2,1)} %param.8) | copy-start | bytes 86404

commit v4 on v3

--- a/solution.py
+++ b/solution.py
@@ -1,3 +1,4 @@
+import functools
 import math
 
 import jax
@@ -12,10 +13,12 @@
 NAMES = ("z_lo", "y", "x", "z_hi", "core")
 DATA = ("z_lo", "y")
 PLANE = ("x", "z_hi")
+CUBE = ("z_lo", "x", "z_hi")
 GROUPS, STEP, SHARE = 4, 40, 96
 LANES = GROUPS * SHARE
 SLOT = 48
 INNER = GROUPS * SLOT
+HALVES, CUT, TAIL = 2, 16, 24
 
 
 def from_behind(value, axes, steps):
@@ -24,7 +27,7 @@
     return lax.ppermute(value, axes, pairs)
 
 
-def vmem_call(kernel, shapes, cost, *operands, scalars=0, scratch=()):
+def vmem_call(kernel, shapes, cost, *operands, mib, scalars=0, scratch=()):
     specs = [
         pl.BlockSpec(memory_space=pltpu.SMEM if place < scalars else pltpu.VMEM)
         for place in range(len(operands))
@@ -35,7 +38,7 @@
         in_specs=specs,
         out_specs=[pl.BlockSpec(memory_space=pltpu.VMEM)] * len(shapes),
         scratch_shapes=list(scratch),
-        compiler_params=pltpu.CompilerParams(vmem_limit_bytes=32 * 1024 * 1024),
+        compiler_params=pltpu.CompilerParams(vmem_limit_bytes=mib * 2**20),
         cost_estimate=pl.CostEstimate(flops=cost[0], bytes_accessed=cost[1], transcendentals=0),
     )(*operands)
 
@@ -52,16 +55,11 @@
         out_ref[place] = parcel
 
 
-def main_kernel(
-    core_ref, act_ref, own_ref, partner_ref, labels_ref, mask_ref, ids_ref,
-    shown_ref, dpre_ref, full_ref, keep_ref, send_ref,
-):
+def unpack(core_ref, own_ref, partner_ref, full_ref):
     first = core_ref[0] == 0
-    count, classes = own_ref.shape[0], shown_ref.shape[1]
     for g in range(GROUPS):
         full_ref[SLOT * g : SLOT * (g + 1)] = jnp.zeros((SLOT, full_ref.shape[1]), jnp.bfloat16)
-
-    for q in range(count // 2):
+    for q in range(own_ref.shape[0] // 2):
         shards = []
         for p in (2 * q, 2 * q + 1):
             own, partner = own_ref[p], partner_ref[p]
@@ -71,6 +69,14 @@
             row = [shard[:, SHARE * g : SHARE * (g + 1)] for shard in shards]
             full_ref[SLOT * g : SLOT * g + STEP, LANES * q : LANES * (q + 1)] = jnp.concatenate(row, axis=1)
 
+
+def main_kernel(
+    core_ref, act_ref, own_ref, partner_ref, labels_ref, mask_ref, ids_ref,
+    shown_ref, dpre_ref, keep_ref, send_ref, full_ref,
+):
+    first = core_ref[0] == 0
+    count, classes = own_ref.shape[0], shown_ref.shape[1]
+    unpack(core_ref, own_ref, partner_ref, full_ref)
     pre = lax.dot_general(
         act_ref[...], full_ref[...], (((1,), (1,)), ((), ())), preferred_element_type=jnp.float32
     )
@@ -91,14 +97,61 @@
             turned, act_ref[:, LANES * q : LANES * (q + 1)], preferred_element_type=jnp.float32
         ).astype(jnp.bfloat16)
         groups = [term[SLOT * g : SLOT * g + STEP] for g in range(GROUPS)]
-        shards = [
-            jnp.concatenate([group[:, SHARE * k : SHARE * (k + 1)] for group in groups], axis=1)
-            for k in range(4)
-        ]
-        for half in range(2):
-            even, odd = shards[2 * half], shards[2 * half + 1]
-            keep_ref[2 * q + half] = jnp.where(first, even, odd)
-            send_ref[2 * q + half] = jnp.where(first, odd, even)
+        for half in range(HALVES):
+            shards = []
+            for k in range(4):
+                lanes = [groups[2 * half + g][:, SHARE * k : SHARE * (k + 1)] for g in range(2)]
+                lanes = jnp.concatenate(lanes, axis=1)
+                tail = lanes[:, 128:]
+                left = tail[CUT:]
+                right = jnp.concatenate([tail[:CUT], jnp.zeros((TAIL - CUT, 64), jnp.bfloat16)], axis=0)
+                shards.append((lanes[:, :128], jnp.concatenate([left, right], axis=1)))
+            for pair in range(2):
+                even, odd = shards[2 * pair], shards[2 * pair + 1]
+                place = 2 * q + pair
+                for rows, e, o in ((slice(0, STEP), even[0], odd[0]), (slice(STEP, STEP + TAIL), even[1], odd[1])):
+                    keep_ref[half, place, rows] = jnp.where(first, e, o)
+                    send_ref[half, place, rows] = jnp.where(first, o, e)
+
+
+def input_kernel(
+    core_ref, act_ref, own_ref, partner_ref, dpre_ref, inverse_ref,
+    out_ref, full_ref, dnorm_ref,
+):
+    unpack(core_ref, own_ref, partner_ref, full_ref)
+    dpre = dpre_ref[...]
+    width = act_ref.shape[1]
+    tiles = [slice(begin, begin + LANES) for begin in range(0, width, LANES)]
+    first = second = 0.0
+    for tile in tiles:
+        dnorm = jnp.dot(dpre, full_ref[:, tile], preferred_element_type=jnp.float32)
+        dnorm_ref[:, tile] = dnorm
+        first += jnp.sum(dnorm, axis=1, keepdims=True)
+        second += jnp.sum(dnorm * act_ref[:, tile].astype(jnp.float32), axis=1, keepdims=True)
+    inverse = inverse_ref[...]
+    first = first * (1.0 / width)
+    second = second * (1.0 / width)
+    for tile in tiles:
+        inner = dnorm_ref[:, tile] - first - act_ref[:, tile].astype(jnp.float32) * second
+        out_ref[:, tile] = (inverse * inner).astype(jnp.bfloat16)
+
+
+def final_kernel(group_ref, weight_ref, gain_ref, weight_grad_ref, gain_grad_ref, *, factor):
+    classes = weight_ref.shape[0]
+    members = group_ref.shape[0] // HALVES
+    parts = []
+    for half in range(HALVES):
+        total = group_ref[half * members].astype(jnp.float32)
+        for member in range(1, members):
+            total += group_ref[half * members + member].astype(jnp.float32)
+        packed = total[STEP:]
+        tail = jnp.concatenate([packed[:CUT, 64:], packed[: STEP - CUT, :64]], axis=0)
+        lanes = jnp.concatenate([total[:STEP], tail], axis=1)
+        parts += [lanes[:, :SHARE], lanes[:, SHARE:]]
+    total = jnp.concatenate(parts, axis=0)[:classes] * factor
+    weight_grad_ref[...] = total * gain_ref[...].astype(jnp.float32)
+    product = total * weight_ref[...].astype(jnp.float32)
+    gain_grad_ref[...] = jnp.sum(product, axis=0, keepdims=True)
 
 
 def parcel_kernel(plan_ref, counts_ref, patches_ref, up_ref, down_ref):
@@ -159,13 +212,15 @@
     peers = X * Z_HI
     core = lax.axis_index("core").astype(jnp.int32)
     wire = jax.ShapeDtypeStruct((peers, STEP, LANES), jnp.bfloat16)
-    (copies,) = vmem_call(prepare_kernel, [wire], (0, 2**20), weight.T, gain[None, :])
+    (copies,) = vmem_call(
+        prepare_kernel, [wire], (0, 2**20), weight.T, gain[None, :], mib=4
+    )
     plane = lax.all_to_all(copies, PLANE, 0, 0)
 
     image = jax.ShapeDtypeStruct((total_rows // counts.shape[0] + 1, width), jnp.bfloat16)
     column = jax.ShapeDtypeStruct((total_rows, 1), jnp.float32)
     up, down = vmem_call(
-        parcel_kernel, [image, image], (0, 3 * 2**20), plan, counts, patches, scalars=2
+        parcel_kernel, [image, image], (0, 3 * 2**20), plan, counts, patches, mib=6, scalars=2
     )
     arrive_low = from_behind(up, DATA, 1)
     arrive_up = from_behind(down, DATA, -1)
@@ -174,48 +229,62 @@
         [jax.ShapeDtypeStruct((total_rows, width), jnp.bfloat16), column, column],
         (10 * total_rows * width, 5 * 2**20),
         plan, counts, patches, arrive_low, arrive_up,
+        mib=14,
         scalars=2,
         scratch=[pltpu.VMEM((total_rows, width), jnp.float32)],
     )
 
+    plane, inverse = lax.optimization_barrier((plane, inverse))
     partner = from_behind(plane, "core", 1)
     slots = jnp.arange(INNER, dtype=jnp.int32)
     ids = (slots // SLOT) * STEP + slots % SLOT
     ids = jnp.where((slots % SLOT < STEP) & (ids < classes), ids, -1)[None, :]
-    shown, dpre, full, keep, send = vmem_call(
+    halves = jax.ShapeDtypeStruct((HALVES, peers, STEP + TAIL, 128), jnp.bfloat16)
+    full = pltpu.VMEM((INNER, width), jnp.bfloat16)
+    shown, dpre, keep, send = vmem_call(
         main_kernel,
         [
             jax.ShapeDtypeStruct((total_rows, classes), jnp.bfloat16),
             jax.ShapeDtypeStruct((total_rows, INNER), jnp.bfloat16),
-            jax.ShapeDtypeStruct((INNER, width), jnp.bfloat16),
-            wire,
-            wire,
+            halves,
+            halves,
         ],
-        (4 * total_rows * width * INNER, 12 * 2**20),
+        (4 * total_rows * width * INNER, 8 * 2**20),
         core[None], act, plane, partner, labels[:, None], mask, ids,
+        mib=20,
         scalars=1,
+        scratch=[full],
     )
     other = from_behind(send, "core", 1)
     chip = (keep.astype(jnp.float32) + other.astype(jnp.float32)).astype(jnp.bfloat16)
-
-    dnorm = jnp.dot(dpre, full, preferred_element_type=jnp.float32)
-    first = jnp.mean(dnorm, axis=1, keepdims=True)
-    normed = act.astype(jnp.float32)
-    second = jnp.mean(dnorm * normed, axis=1, keepdims=True)
-    input_grad = (inverse * (dnorm - first - normed * second)).astype(jnp.bfloat16)
-
-    owned = lax.all_to_all(chip, PLANE, 0, 0)
+    chip, dpre = lax.optimization_barrier((chip, dpre))
+    (input_grad,) = vmem_call(
+        input_kernel,
+        [jax.ShapeDtypeStruct((total_rows, width), jnp.bfloat16)],
+        (2 * total_rows * width * INNER, 6 * 2**20),
+        core[None], act, plane, partner, dpre, inverse,
+        mib=20,
+        scalars=1,
+        scratch=[full, pltpu.VMEM((total_rows, width), jnp.float32)],
+    )
+
+    owned = lax.all_to_all(chip.reshape(HALVES * peers, STEP + TAIL, 128), CUBE, 0, 0)
+    owned, input_grad = lax.optimization_barrier((owned, input_grad))
     owned = jnp.sum(owned.astype(jnp.float32), axis=0).astype(jnp.bfloat16)
     group = jnp.broadcast_to(owned[None], (Z_LO * Y,) + owned.shape)
     group = lax.all_to_all(group, DATA, 0, 0)
-    total = jnp.sum(group.astype(jnp.float32), axis=0)
-    total = total.reshape(STEP, GROUPS, share).transpose(1, 0, 2).reshape(GROUPS * STEP, share)
-    total = total[:classes]
     factor = 1.0 / math.sqrt(total_rows * Z_LO * Y * X * Z_HI * CORE)
-    gain32 = gain.astype(jnp.float32)[None, :]
-    weight_grad = (total * (gain32 * factor)).T
-    gain_grad = jnp.sum(weight.T.astype(jnp.float32) * total, axis=0) * factor
-    return (shown, input_grad, weight_grad, gain_grad)
+    weight_grad, gain_grad = vmem_call(
+        functools.partial(final_kernel, factor=factor),
+        [
+            jax.ShapeDtypeStruct((classes, share), jnp.float32),
+            jax.ShapeDtypeStruct((1, share), jnp.float32),
+        ],
+        (0, 2**20),
+        group, weight.T, gain[None, :],
+        mib=4,
+    )
+    return (shown, input_grad, weight_grad.T, gain_grad[0])
 
 
 def solution(mesh):

time: 154 us -> 136 us (0.88)
  the two profiles are of different devices: /device:TPU:20 before, /device:TPU:18 now
where the time goes in v4:
time: 136 us; the launch traced here: 135 us
  waiting for transfers between devices  47.6 us (35%)
  starting transfers between devices  39.5 us (29%)
  blocking collectives  26.5 us (19%)
  Pallas kernels  11.3 us (8%)
  local copies, waits for them, and re-layouts  6.91 us (5%)
  other arithmetic  2.78 us (2%)
    all_to_all x1, blocking collectives, body(): group = lax.all_to_all(group, DATA, 0, 0)  26.5 us
    all_to_all x1, waiting for transfers between devices, body(): lax.all_to_all(chip.reshape(HALVES * peers, STEP + TAIL, 128), CUBE, 0, 0)  24.1 us
    all_to_all x1, starting transfers between devices, body(): plane = lax.all_to_all(copies, PLANE, 0, 0)  21.4 us
    ppermute x4, waiting for transfers between devices, from_behind(): return lax.ppermute(value, axes, pairs)  16.7 us
    pallas_call x6, Pallas kernels, vmem_call(): pl.pallas_call(kernel, out_shape=shapes, in_specs=specs, out_specs=[pl.Bl...  11.3 us
    ppermute x4, starting transfers between devices, from_behind(): return lax.ppermute(value, axes, pairs)  9.79 us
    all_to_all x1, starting transfers between devices, body(): lax.all_to_all(chip.reshape(HALVES * peers, STEP + TAIL, 128), CUBE, 0, 0)  8.28 us
    all_to_all x1, waiting for transfers between devices, body(): plane = lax.all_to_all(copies, PLANE, 0, 0)  6.82 us
  transfers between devices with their start and end apart: 6, of which 6 were waited for; matrix products, arithmetic and copies ran while one was open for 0% of the time, Pallas kernels for 5%

profile of v4, /device:TPU:18, one launch (start us, length us, event | category | flops | bytes accessed | tf_op | source)
XLA Modules:
  0.0 135.3 jit_solution(3498375087694401331)
XLA Ops:
  0.7 0.9 copy-done.7
  2.4 0.9 copy-done.6
  3.3 21.4 %all-to-all-start = ((bf16[32,40,384]{2,1,0:T(8,128)(2,1)}), bf16[32,40,384]{2,1,0:T(8,128)(2,1)S(1)}, u32[]{:S(2)}, u32[]{:S(2)}) async-start(bf16[32,40,384]{2,1,0:T(8,128)(2,1)} %copy-done.6), calls=%async_computation | async-start | bytes 1966080 | tf_op jit(solution)/shard_map/all_to_all | solution.py:218
  25.5 3.7 %collective-permute-start = (bf16[37,6144]{1,0:T(8,128)(2,1)S(1)}, bf16[37,6144]{1,0:T(8,128)(2,1)S(1)}, u32[]{:S(2)}, u32[]{:S(2)}) collective-permute-start(bf16[37,6144]{1,0:T(8,128)(2,1)S(1)} %get-tuple-element.21), channel_id=1, source_target_pairs={{0,64},{64,128},{128,192},{192,256},{256,320},{320,384},{384,448},... | collective-permute-start | bytes 1363976 | tf_op jit(solution)/shard_map/ppermute | solution.py:27
  29.2 2.1 %collective-permute-start.1 = (bf16[37,6144]{1,0:T(8,128)(2,1)S(1)}, bf16[37,6144]{1,0:T(8,128)(2,1)S(1)}, u32[]{:S(2)}, u32[]{:S(2)}) collective-permute-start(bf16[37,6144]{1,0:T(8,128)(2,1)S(1)} %get-tuple-element.22), channel_id=1, source_target_pairs={{0,960},{64,0},{128,64},{192,128},{256,192},{320,256},{384,320},{4... | collective-permute-start | bytes 1363976 | tf_op jit(solution)/shard_map/ppermute | solution.py:27
  31.3 8.5 %collective-permute-done.low_ref = bf16[37,6144]{1,0:T(8,128)(2,1)S(1)} collective-permute-done((bf16[37,6144]{1,0:T(8,128)(2,1)S(1)}, bf16[37,6144]{1,0:T(8,128)(2,1)S(1)}, u32[]{:S(2)}, u32[]{:S(2)}) %collective-permute-start) | collective-permute-done | bytes 454688 | tf_op jit(solution)/shard_map/ppermute | solution.py:27
  39.8 3.3 %collective-permute-done.1.high_ref = bf16[37,6144]{1,0:T(8,128)(2,1)S(1)} collective-permute-done((bf16[37,6144]{1,0:T(8,128)(2,1)S(1)}, bf16[37,6144]{1,0:T(8,128)(2,1)S(1)}, u32[]{:S(2)}, u32[]{:S(2)}) %collective-permute-start.1) | collective-permute-done | bytes 454688 | tf_op jit(solution)/shard_map/ppermute | solution.py:27
  43.1 1.9 %shard_map.94 = (bf16[144,6144]{1,0:T(8,128)(2,1)S(1)}, f32[144,1]{1,0:T(8,128)S(1)}, f32[144,1]{1,0:T(8,128)S(1)}) custom-call(s32[1,2]{1,0:T(1,128)S(1)} %copy-done.11, s32[4]{0:T(128)S(1)} %copy-done.12, bf16[144,6144]{1,0:T(8,128)(2,1)S(1)} %copy-done, bf16[37,6144]{1,0:T(8,128)(2,1)S(1)} %collective-permute-done.low_ref, ...), custom_call_target="tpu_custom_call" | custom-call | flops 8847360 | bytes 5242880 | tf_op jit(solution)/shard_map/pallas_call | solution.py:35
  45.0 1.2 copy-done.1
  46.2 6.8 %all-to-all-done.own_ref = bf16[32,40,384]{2,1,0:T(8,128)(2,1)S(1)} async-done(((bf16[32,40,384]{2,1,0:T(8,128)(2,1)}), bf16[32,40,384]{2,1,0:T(8,128)(2,1)S(1)}, u32[]{:S(2)}, u32[]{:S(2)}) %all-to-all-start) | async-done | bytes 983072 | tf_op jit(solution)/shard_map/all_to_all | solution.py:218
  53.0 1.9 %collective-permute-start.2 = (bf16[32,40,384]{2,1,0:T(8,128)(2,1)S(1)}, bf16[32,40,384]{2,1,0:T(8,128)(2,1)S(1)}, u32[]{:S(2)}, u32[]{:S(2)}) collective-permute-start(bf16[32,40,384]{2,1,0:T(8,128)(2,1)S(1)} %all-to-all-done.own_ref), channel_id=1, source_target_pairs={{0,1},{1,0},{2,3},{3,2},{4,5},{5,4},{6,7},{7,6},{8,9},{9,8},{10,11... | collective-permute-start | bytes 2949128 | tf_op jit(solution)/shard_map/ppermute | solution.py:27
  55.1 2.4 %collective-permute-done.2.partner_ref = bf16[32,40,384]{2,1,0:T(8,128)(2,1)S(1)} collective-permute-done((bf16[32,40,384]{2,1,0:T(8,128)(2,1)S(1)}, bf16[32,40,384]{2,1,0:T(8,128)(2,1)S(1)}, u32[]{:S(2)}, u32[]{:S(2)}) %collective-permute-start.2) | collective-permute-done | bytes 983072 | tf_op jit(solution)/shard_map/ppermute | solution.py:27
  57.5 1.8 %copy-done.2 = bf16[144,6144]{1,0:T(8,128)(2,1)S(1)} copy-done((bf16[144,6144]{1,0:T(8,128)(2,1)S(1)}, bf16[144,6144]{1,0:T(8,128)(2,1)}, u32[]{:S(2)}) %copy-start.2) | copy-done | bytes 1769496
  59.3 3.5 %shard_map.96 = (bf16[144,150]{1,0:T(8,128)(2,1)}, bf16[144,192]{1,0:T(8,128)(2,1)S(1)}, bf16[2,32,64,128]{3,2,1,0:T(8,128)(2,1)S(1)}, bf16[2,32,64,128]{3,2,1,0:T(8,128)(2,1)S(1)}) custom-call(s32[1]{0:T(128)} %bitcast.core_ref, bf16[144,6144]{1,0:T(8,128)(2,1)S(1)} %copy-done.2, bf16[32,40,384]{2,1,0:T(8,128)(2,1)S(1)} %all-to-all-done.own_ref, ...), custom_call_target="tpu_custom_call" | custom-call | flops 679477248 | bytes 8388608 | tf_op jit(solution)/shard_map/pallas_call | solution.py:35
  62.8 2.0 %collective-permute-start.3 = (bf16[2,32,64,128]{3,2,1,0:T(8,128)(2,1)S(1)}, bf16[2,32,64,128]{3,2,1,0:T(8,128)(2,1)S(1)}, u32[]{:S(2)}, u32[]{:S(2)}) collective-permute-start(bf16[2,32,64,128]{3,2,1,0:T(8,128)(2,1)S(1)} %get-tuple-element.29), channel_id=1, source_target_pairs={{0,1},{1,0},{2,3},{3,2},{4,5},{5,4},{6,7},{7,6},{8,9},{9,8},{10,11... | collective-permute-start | bytes 3145736 | tf_op jit(solution)/shard_map/ppermute | solution.py:27
  64.8 2.5 %collective-permute-done.3 = bf16[2,32,64,128]{3,2,1,0:T(8,128)(2,1)S(1)} collective-permute-done((bf16[2,32,64,128]{3,2,1,0:T(8,128)(2,1)S(1)}, bf16[2,32,64,128]{3,2,1,0:T(8,128)(2,1)S(1)}, u32[]{:S(2)}, u32[]{:S(2)}) %collective-permute-start.3) | collective-permute-done | bytes 1048608 | tf_op jit(solution)/shard_map/ppermute | solution.py:27
  67.3 1.4 %add_convert_fusion = bf16[2,32,64,128]{3,2,1,0:T(8,128)(2,1)} fusion(bf16[2,32,64,128]{3,2,1,0:T(8,128)(2,1)S(1)} %collective-permute-done.3, bf16[2,32,64,128]{3,2,1,0:T(8,128)(2,1)S(1)} %get-tuple-element.28), kind=kLoop, calls=%fused_computation | loop fusion | flops 2097152 | bytes 3145728 | tf_op jit(solution)/shard_map/convert_element_type | solution.py:259
  68.7 8.3 %all-to-all-start.1 = ((bf16[64,64,128]{2,1,0:T(8,128)(2,1)}), bf16[64,64,128]{2,1,0:T(8,128)(2,1)}, u32[]{:S(2)}, u32[]{:S(2)}) async-start(bf16[64,64,128]{2,1,0:T(8,128)(2,1)} %bitcast.11), calls=%async_computation.1 | async-start | bytes 2097152 | tf_op jit(solution)/shard_map/all_to_all | solution.py:271
  77.0 1.2 copy-done.5
  78.2 4.2 %shard_map.97 = bf16[144,6144]{1,0:T(8,128)(2,1)} custom-call(s32[1]{0:T(128)} %bitcast.core_ref, bf16[144,6144]{1,0:T(8,128)(2,1)S(1)} %copy-done.3, bf16[32,40,384]{2,1,0:T(8,128)(2,1)S(1)} %all-to-all-done.own_ref, bf16[32,40,384]{2,1,0:T(8,128)(2,1)S(1)} %copy-done.5, bf16[144,192]{1,0:T(8,128)(2,1)S(1)} %get-tuple-element.32.dpre_ref, ...), custom_call_target="tpu_custom_call" | custom-call | flops 339738624 | bytes 6291456 | tf_op jit(solution)/shard_map/pallas_call | solution.py:35
  82.4 24.1 %all-to-all-done.1 = bf16[64,64,128]{2,1,0:T(8,128)(2,1)} async-done(((bf16[64,64,128]{2,1,0:T(8,128)(2,1)}), bf16[64,64,128]{2,1,0:T(8,128)(2,1)}, u32[]{:S(2)}, u32[]{:S(2)}) %all-to-all-start.1) | async-done | bytes 1048608 | tf_op jit(solution)/shard_map/all_to_all | solution.py:271
  106.5 1.4 %reduce_sum.12 = bf16[64,128]{1,0:T(8,128)(2,1)S(1)} reduce(bf16[64,64,128]{2,1,0:T(8,128)(2,1)} %all-to-all-done.1, bf16[]{:T(256)} %constant.34.clone.1), dimensions={0}, to_apply=%region_0.1 | reduce | flops 516096 | bytes 1064962 | tf_op jit(solution)/shard_map/reduce_sum | solution.py:273
  108.0 26.5 %all_to_all.15.group_ref = bf16[16,64,128]{2,1,0:T(8,128)(2,1)S(1)} all-to-all(bf16[16,64,128]{2,1,0:T(8,128)(2,1)S(1)} %broadcast_in_dim.23), channel_id=1, replica_groups=mesh['z_lo'=2,'y'=8,'x'=8,'z_hi'=4,'core'=2] {'z_lo','y'}, dimensions={0} | all-to-all | bytes 524288 | tf_op jit(solution)/shard_map/all_to_all | solution.py:275
  134.4 0.9 shard_map.98
  (28 shorter events, 1.7 us)
Async XLA Ops:
  0.6 24.1 %copy-start = (bf16[144,6144]{1,0:T(8,128)(2,1)S(1)}, bf16[144,6144]{1,0:T(8,128)(2,1)}, u32[]{:S(2)}) copy-start(bf16[144,6144]{1,0:T(8,128)(2,1)} %patches_ref.3) | copy-start | bytes 5308420
  0.6 0.9 copy-start.7
  1.5 0.7 copy-start.9
  2.2 22.5 %copy-start.11 = (s32[1,2]{1,0:T(1,128)S(1)}, s32[1,2]{1,0:T(1,128)}, u32[]{:S(2)}) copy-start(s32[1,2]{1,0:T(1,128)} %plan_ref.3) | copy-start | bytes 28
  2.2 22.5 %copy-start.12 = (s32[4]{0:T(128)S(1)}, s32[4]{0:T(128)}, u32[]{:S(2)}) copy-start(s32[4]{0:T(128)} %counts_ref.3) | copy-start | bytes 52
  2.4 1.0 copy-start.6
  3.3 49.7 %all-to-all-start = ((bf16[32,40,384]{2,1,0:T(8,128)(2,1)}), bf16[32,40,384]{2,1,0:T(8,128)(2,1)S(1)}, u32[]{:S(2)}, u32[]{:S(2)}) async-start(bf16[32,40,384]{2,1,0:T(8,128)(2,1)} %copy-done.6), calls=%async_computation | async-start | bytes 1966080 | tf_op jit(solution)/shard_map/all_to_all | solution.py:218
  25.4 29.5 %copy-start.13 = (s32[144]{0:T(256)S(1)}, s32[144]{0:T(256)}, u32[]{:S(2)}) copy-start(s32[144]{0:T(256)} %param.7) | copy-start | bytes 1732
  25.5 14.4 %collective-permute-start = (bf16[37,6144]{1,0:T(8,128)(2,1)S(1)}, bf16[37,6144]{1,0:T(8,128)(2,1)S(1)}, u32[]{:S(2)}, u32[]{:S(2)}) collective-permute-start(bf16[37,6144]{1,0:T(8,128)(2,1)S(1)} %get-tuple-element.21), channel_id=1, source_target_pairs={{0,64},{64,128},{128,192},{192,256},{256,320},{320,384},{384,448},... | collective-permute-start | bytes 1363976 | tf_op jit(solution)/shard_map/ppermute | solution.py:27
  29.2 13.9 %collective-permute-start.1 = (bf16[37,6144]{1,0:T(8,128)(2,1)S(1)}, bf16[37,6144]{1,0:T(8,128)(2,1)S(1)}, u32[]{:S(2)}, u32[]{:S(2)}) collective-permute-start(bf16[37,6144]{1,0:T(8,128)(2,1)S(1)} %get-tuple-element.22), channel_id=1, source_target_pairs={{0,960},{64,0},{128,64},{192,128},{256,192},{320,256},{384,320},{4... | collective-permute-start | bytes 1363976 | tf_op jit(solution)/shard_map/ppermute | solution.py:27
  45.0 1.2 copy-start.1
  53.0 4.4 %collective-permute-start.2 = (bf16[32,40,384]{2,1,0:T(8,128)(2,1)S(1)}, bf16[32,40,384]{2,1,0:T(8,128)(2,1)S(1)}, u32[]{:S(2)}, u32[]{:S(2)}) collective-permute-start(bf16[32,40,384]{2,1,0:T(8,128)(2,1)S(1)} %all-to-all-done.own_ref), channel_id=1, source_target_pairs={{0,1},{1,0},{2,3},{3,2},{4,5},{5,4},{6,7},{7,6},{8,9},{9,8},{10,11... | collective-permute-start | bytes 2949128 | tf_op jit(solution)/shard_map/ppermute | solution.py:27
  57.4 5.3 %copy-start.4 = (bf16[32,40,384]{2,1,0:T(8,128)(2,1)}, bf16[32,40,384]{2,1,0:T(8,128)(2,1)S(1)}, u32[]{:S(2)}) copy-start(bf16[32,40,384]{2,1,0:T(8,128)(2,1)S(1)} %collective-permute-done.2.partner_ref) | copy-start | bytes 2949124
  57.4 1.8 %copy-start.2 = (bf16[144,6144]{1,0:T(8,128)(2,1)S(1)}, bf16[144,6144]{1,0:T(8,128)(2,1)}, u32[]{:S(2)}) copy-start(bf16[144,6144]{1,0:T(8,128)(2,1)} %copy-done.1) | copy-start | bytes 5308420
  62.8 4.6 %collective-permute-start.3 = (bf16[2,32,64,128]{3,2,1,0:T(8,128)(2,1)S(1)}, bf16[2,32,64,128]{3,2,1,0:T(8,128)(2,1)S(1)}, u32[]{:S(2)}, u32[]{:S(2)}) collective-permute-start(bf16[2,32,64,128]{3,2,1,0:T(8,128)(2,1)S(1)} %get-tuple-element.29), channel_id=1, source_target_pairs={{0,1},{1,0},{2,3},{3,2},{4,5},{5,4},{6,7},{7,6},{8,9},{9,8},{10,11... | collective-permute-start | bytes 3145736 | tf_op jit(solution)/shard_map/ppermute | solution.py:27
  68.7 8.3 %copy-start.3 = (bf16[144,6144]{1,0:T(8,128)(2,1)S(1)}, bf16[144,6144]{1,0:T(8,128)(2,1)}, u32[]{:S(2)}) copy-start(bf16[144,6144]{1,0:T(8,128)(2,1)} %copy-done.1) | copy-start | bytes 5308420
  68.7 37.8 %all-to-all-start.1 = ((bf16[64,64,128]{2,1,0:T(8,128)(2,1)}), bf16[64,64,128]{2,1,0:T(8,128)(2,1)}, u32[]{:S(2)}, u32[]{:S(2)}) async-start(bf16[64,64,128]{2,1,0:T(8,128)(2,1)} %bitcast.11), calls=%async_computation.1 | async-start | bytes 2097152 | tf_op jit(solution)/shard_map/all_to_all | solution.py:271
  77.0 1.2 copy-start.5
  82.4 52.0 %copy-start.8 = (bf16[96,150]{0,1:T(8,128)(2,1)S(1)}, bf16[96,150]{0,1:T(8,128)(2,1)}, u32[]{:S(2)}) copy-start(bf16[96,150]{0,1:T(8,128)(2,1)} %param.8) | copy-start | bytes 86404
  82.4 52.0 %copy-start.10 = (bf16[96]{0:T(256)(128)(2,1)S(1)}, bf16[96]{0:T(256)(128)(2,1)}, u32[]{:S(2)}) copy-start(bf16[96]{0:T(256)(128)(2,1)} %param.9) | copy-start | bytes 580

commit v5 on v4

--- a/solution.py
+++ b/solution.py
@@ -227,7 +227,7 @@
     act, inverse, mask = vmem_call(
         norm_kernel,
         [jax.ShapeDtypeStruct((total_rows, width), jnp.bfloat16), column, column],
-        (10 * total_rows * width, 5 * 2**20),
+        (2**37, 5 * 2**20),
         plan, counts, patches, arrive_low, arrive_up,
         mib=14,
         scalars=2,

time: 136 us -> 136 us (level)
  blocking collectives: 26.5 us -> 18.8 us
  Pallas kernels: 11.3 us -> 15.6 us
  waiting for transfers between devices: 47.6 us -> 49.7 us
    all_to_all x1, waiting for transfers between devices: 6.82 us -> 20.5 us  [body(): plane = lax.all_to_all(copies, PLANE, 0, 0)]
    ppermute x4, waiting for transfers between devices: 16.7 us -> 5.03 us  [from_behind(): return lax.ppermute(value, axes, pairs)]
    all_to_all x1, blocking collectives: 26.5 us -> 18.8 us  [body(): group = lax.all_to_all(group, DATA, 0, 0)]
    pallas_call x6, Pallas kernels: 11.3 us -> 15.6 us  [vmem_call(): pl.pallas_call(kernel, out_shape=shapes, in_specs=specs, out_specs=[pl.Bl...]
    unnamed x28 -> x26, local copies, waits for them, and re-layouts: 6.76 us -> 7.9 us
  transfers between devices with their start and end apart: 6 -> 6, of which waited for: 6 -> 4; matrix products, arithmetic and copies ran while one was open for 0% -> 0% of each run, Pallas kernels for 5% -> 6%
where the time goes in v5:
time: 136 us; the launch traced here: 135 us
  waiting for transfers between devices  49.7 us (37%)
  starting transfers between devices  39.7 us (29%)
  blocking collectives  18.8 us (14%)
  Pallas kernels  15.6 us (11%)
  local copies, waits for them, and re-layouts  8.05 us (6%)
  other arithmetic  2.79 us (2%)
    all_to_all x1, waiting for transfers between devices, body(): lax.all_to_all(chip.reshape(HALVES * peers, STEP + TAIL, 128), CUBE, 0, 0)  24.1 us
    all_to_all x1, starting transfers between devices, body(): plane = lax.all_to_all(copies, PLANE, 0, 0)  21.6 us
    all_to_all x1, waiting for transfers between devices, body(): plane = lax.all_to_all(copies, PLANE, 0, 0)  20.5 us
    all_to_all x1, blocking collectives, body(): group = lax.all_to_all(group, DATA, 0, 0)  18.8 us
    pallas_call x6, Pallas kernels, vmem_call(): pl.pallas_call(kernel, out_shape=shapes, in_specs=specs, out_specs=[pl.Bl...  15.6 us
    ppermute x4, starting transfers between devices, from_behind(): return lax.ppermute(value, axes, pairs)  9.91 us
    all_to_all x1, starting transfers between devices, body(): lax.all_to_all(chip.reshape(HALVES * peers, STEP + TAIL, 128), CUBE, 0, 0)  8.21 us
    unnamed x26, local copies, waits for them, and re-layouts  7.9 us
  transfers between devices with their start and end apart: 6, of which 4 were waited for; matrix products, arithmetic and copies ran while one was open for 0% of the time, Pallas kernels for 6%

profile of v5, /device:TPU:18, one launch (start us, length us, event | category | flops | bytes accessed | tf_op | source)
XLA Modules:
  0.0 135.3 jit_solution(15779112738535876630)
XLA Ops:
  0.6 1.5 %copy-done = bf16[144,6144]{1,0:T(8,128)(2,1)S(1)} copy-done((bf16[144,6144]{1,0:T(8,128)(2,1)S(1)}, bf16[144,6144]{1,0:T(8,128)(2,1)}, u32[]{:S(2)}) %copy-start) | copy-done | bytes 1769496
  3.4 1.5 %shard_map.93 = (bf16[37,6144]{1,0:T(8,128)(2,1)}, bf16[37,6144]{1,0:T(8,128)(2,1)S(1)}) custom-call(s32[1,2]{1,0:T(1,128)S(1)} %copy-done.4, s32[4]{0:T(128)S(1)} %copy-done.6, bf16[144,6144]{1,0:T(8,128)(2,1)S(1)} %copy-done), custom_call_target="tpu_custom_call" | custom-call | bytes 3145728 | tf_op jit(solution)/shard_map/pallas_call | solution.py:35
  5.0 3.7 %collective-permute-start = (bf16[37,6144]{1,0:T(8,128)(2,1)}, bf16[37,6144]{1,0:T(8,128)(2,1)S(1)}, u32[]{:S(2)}, u32[]{:S(2)}) collective-permute-start(bf16[37,6144]{1,0:T(8,128)(2,1)} %get-tuple-element.21), channel_id=1, source_target_pairs={{0,64},{64,128},{128,192},{192,256},{256,320},{320,384},{384,448},... | collective-permute-start | bytes 1363976 | tf_op jit(solution)/shard_map/ppermute | solution.py:27
  8.7 2.2 %collective-permute-start.1 = (bf16[37,6144]{1,0:T(8,128)(2,1)S(1)}, bf16[37,6144]{1,0:T(8,128)(2,1)S(1)}, u32[]{:S(2)}, u32[]{:S(2)}) collective-permute-start(bf16[37,6144]{1,0:T(8,128)(2,1)S(1)} %get-tuple-element.22), channel_id=1, source_target_pairs={{0,960},{64,0},{128,64},{192,128},{256,192},{320,256},{384,320},{4... | collective-permute-start | bytes 1363976 | tf_op jit(solution)/shard_map/ppermute | solution.py:27
  11.0 1.1 shard_map.95
  12.1 21.6 %all-to-all-start = ((bf16[32,40,384]{2,1,0:T(8,128)(2,1)}), bf16[32,40,384]{2,1,0:T(8,128)(2,1)S(1)}, u32[]{:S(2)}, u32[]{:S(2)}) async-start(bf16[32,40,384]{2,1,0:T(8,128)(2,1)} %shard_map.95), calls=%async_computation | async-start | bytes 1966080 | tf_op jit(solution)/shard_map/all_to_all | solution.py:218
  34.5 0.8 copy-done.10
  35.3 1.5 %copy-done.1 = bf16[144,6144]{1,0:T(8,128)(2,1)S(1)} copy-done((bf16[144,6144]{1,0:T(8,128)(2,1)S(1)}, bf16[144,6144]{1,0:T(8,128)(2,1)}, u32[]{:S(2)}) %copy-start.1) | copy-done | bytes 1769496
  36.7 1.0 copy-done.9
  37.8 1.0 copy-done.11
  38.8 1.9 %shard_map.94 = (bf16[144,6144]{1,0:T(8,128)(2,1)S(1)}, f32[144,1]{1,0:T(8,128)S(1)}, f32[144,1]{1,0:T(8,128)S(1)}) custom-call(s32[1,2]{1,0:T(1,128)S(1)} %copy-done.5, s32[4]{0:T(128)S(1)} %copy-done.7, bf16[144,6144]{1,0:T(8,128)(2,1)S(1)} %copy-done.1, bf16[37,6144]{1,0:T(8,128)(2,1)S(1)} %copy-done.9, bf16[37,6144]{1,0:T(8,128)(2,1)S(1)} %copy-done.11), custom_call_target="tpu_custom_call" | custom-call | flops 137438953472 | bytes 5242880 | tf_op jit(solution)/shard_map/pallas_call | solution.py:35
  40.7 20.5 %all-to-all-done.own_ref = bf16[32,40,384]{2,1,0:T(8,128)(2,1)S(1)} async-done(((bf16[32,40,384]{2,1,0:T(8,128)(2,1)}), bf16[32,40,384]{2,1,0:T(8,128)(2,1)S(1)}, u32[]{:S(2)}, u32[]{:S(2)}) %all-to-all-start) | async-done | bytes 983072 | tf_op jit(solution)/shard_map/all_to_all | solution.py:218
  61.3 1.9 %collective-permute-start.2 = (bf16[32,40,384]{2,1,0:T(8,128)(2,1)S(1)}, bf16[32,40,384]{2,1,0:T(8,128)(2,1)}, u32[]{:S(2)}, u32[]{:S(2)}) collective-permute-start(bf16[32,40,384]{2,1,0:T(8,128)(2,1)S(1)} %all-to-all-done.own_ref), channel_id=1, source_target_pairs={{0,1},{1,0},{2,3},{3,2},{4,5},{5,4},{6,7},{7,6},{8,9},{9,8},{10,11... | collective-permute-start | bytes 2949128 | tf_op jit(solution)/shard_map/ppermute | solution.py:27
  63.3 2.5 %collective-permute-done.2.partner_ref = bf16[32,40,384]{2,1,0:T(8,128)(2,1)} collective-permute-done((bf16[32,40,384]{2,1,0:T(8,128)(2,1)S(1)}, bf16[32,40,384]{2,1,0:T(8,128)(2,1)}, u32[]{:S(2)}, u32[]{:S(2)}) %collective-permute-start.2) | collective-permute-done | bytes 983072 | tf_op jit(solution)/shard_map/ppermute | solution.py:27
  65.8 4.7 %shard_map.96 = (bf16[144,150]{1,0:T(8,128)(2,1)}, bf16[144,192]{1,0:T(8,128)(2,1)S(1)}, bf16[2,32,64,128]{3,2,1,0:T(8,128)(2,1)S(1)}, bf16[2,32,64,128]{3,2,1,0:T(8,128)(2,1)S(1)}) custom-call(s32[1]{0:T(128)} %bitcast.core_ref, bf16[144,6144]{1,0:T(8,128)(2,1)S(1)} %get-tuple-element.23.act_ref, bf16[32,40,384]{2,1,0:T(8,128)(2,1)S(1)} %all-to-all-done.own_ref, ...), custom_call_target="tpu_custom_call" | custom-call | flops 679477248 | bytes 8388608 | tf_op jit(solution)/shard_map/pallas_call | solution.py:35
  70.5 2.0 %collective-permute-start.3 = (bf16[2,32,64,128]{3,2,1,0:T(8,128)(2,1)S(1)}, bf16[2,32,64,128]{3,2,1,0:T(8,128)(2,1)S(1)}, u32[]{:S(2)}, u32[]{:S(2)}) collective-permute-start(bf16[2,32,64,128]{3,2,1,0:T(8,128)(2,1)S(1)} %get-tuple-element.29), channel_id=1, source_target_pairs={{0,1},{1,0},{2,3},{3,2},{4,5},{5,4},{6,7},{7,6},{8,9},{9,8},{10,11... | collective-permute-start | bytes 3145736 | tf_op jit(solution)/shard_map/ppermute | solution.py:27
  72.6 2.5 %collective-permute-done.3 = bf16[2,32,64,128]{3,2,1,0:T(8,128)(2,1)S(1)} collective-permute-done((bf16[2,32,64,128]{3,2,1,0:T(8,128)(2,1)S(1)}, bf16[2,32,64,128]{3,2,1,0:T(8,128)(2,1)S(1)}, u32[]{:S(2)}, u32[]{:S(2)}) %collective-permute-start.3) | collective-permute-done | bytes 1048608 | tf_op jit(solution)/shard_map/ppermute | solution.py:27
  75.1 1.4 %add_convert_fusion = bf16[2,32,64,128]{3,2,1,0:T(8,128)(2,1)} fusion(bf16[2,32,64,128]{3,2,1,0:T(8,128)(2,1)S(1)} %collective-permute-done.3, bf16[2,32,64,128]{3,2,1,0:T(8,128)(2,1)S(1)} %get-tuple-element.28), kind=kLoop, calls=%fused_computation | loop fusion | flops 2097152 | bytes 3145728 | tf_op jit(solution)/shard_map/convert_element_type | solution.py:259
  76.5 8.2 %all-to-all-start.1 = ((bf16[64,64,128]{2,1,0:T(8,128)(2,1)}), bf16[64,64,128]{2,1,0:T(8,128)(2,1)}, u32[]{:S(2)}, u32[]{:S(2)}) async-start(bf16[64,64,128]{2,1,0:T(8,128)(2,1)} %bitcast.11), calls=%async_computation.1 | async-start | bytes 2097152 | tf_op jit(solution)/shard_map/all_to_all | solution.py:271
  84.7 5.5 %shard_map.97 = bf16[144,6144]{1,0:T(8,128)(2,1)} custom-call(s32[1]{0:T(128)} %bitcast.core_ref, bf16[144,6144]{1,0:T(8,128)(2,1)S(1)} %get-tuple-element.23.act_ref, bf16[32,40,384]{2,1,0:T(8,128)(2,1)S(1)} %all-to-all-done.own_ref, bf16[32,40,384]{2,1,0:T(8,128)(2,1)} %collective-permute-done.2.partner_ref, ...), custom_call_target="tpu_custom_call" | custom-call | flops 339738624 | bytes 6291456 | tf_op jit(solution)/shard_map/pallas_call | solution.py:35
  90.1 24.1 %all-to-all-done.1 = bf16[64,64,128]{2,1,0:T(8,128)(2,1)} async-done(((bf16[64,64,128]{2,1,0:T(8,128)(2,1)}), bf16[64,64,128]{2,1,0:T(8,128)(2,1)}, u32[]{:S(2)}, u32[]{:S(2)}) %all-to-all-start.1) | async-done | bytes 1048608 | tf_op jit(solution)/shard_map/all_to_all | solution.py:271
  114.2 1.4 %reduce_sum.12 = bf16[64,128]{1,0:T(8,128)(2,1)S(1)} reduce(bf16[64,64,128]{2,1,0:T(8,128)(2,1)} %all-to-all-done.1, bf16[]{:T(256)} %constant.34.clone.1), dimensions={0}, to_apply=%region_0.1 | reduce | flops 516096 | bytes 1064962 | tf_op jit(solution)/shard_map/reduce_sum | solution.py:273
  115.7 18.8 %all_to_all.15.group_ref = bf16[16,64,128]{2,1,0:T(8,128)(2,1)S(1)} all-to-all(bf16[16,64,128]{2,1,0:T(8,128)(2,1)S(1)} %broadcast_in_dim.23), channel_id=1, replica_groups=mesh['z_lo'=2,'y'=8,'x'=8,'z_hi'=4,'core'=2] {'z_lo','y'}, dimensions={0} | all-to-all | bytes 524288 | tf_op jit(solution)/shard_map/all_to_all | solution.py:275
  134.5 0.9 shard_map.98
  (26 shorter events, 2.3 us)
Async XLA Ops:
  0.6 1.5 %copy-start = (bf16[144,6144]{1,0:T(8,128)(2,1)S(1)}, bf16[144,6144]{1,0:T(8,128)(2,1)}, u32[]{:S(2)}) copy-start(bf16[144,6144]{1,0:T(8,128)(2,1)} %patches_ref.3) | copy-start | bytes 5308420
  2.1 0.7 copy-start.4
  2.8 0.7 copy-start.6
  3.4 7.5 %copy-start.2 = (bf16[96,150]{0,1:T(8,128)(2,1)S(1)}, bf16[96,150]{0,1:T(8,128)(2,1)}, u32[]{:S(2)}) copy-start(bf16[96,150]{0,1:T(8,128)(2,1)} %param.8) | copy-start | bytes 86404
  3.4 7.5 %copy-start.3 = (bf16[96]{0:T(256)(128)(2,1)S(1)}, bf16[96]{0:T(256)(128)(2,1)}, u32[]{:S(2)}) copy-start(bf16[96]{0:T(256)(128)(2,1)} %param.9) | copy-start | bytes 580
  5.0 30.3 %copy-start.5 = (s32[1,2]{1,0:T(1,128)S(1)}, s32[1,2]{1,0:T(1,128)}, u32[]{:S(2)}) copy-start(s32[1,2]{1,0:T(1,128)} %plan_ref.3) | copy-start | bytes 28
  5.0 30.3 %copy-start.7 = (s32[4]{0:T(128)S(1)}, s32[4]{0:T(128)}, u32[]{:S(2)}) copy-start(s32[4]{0:T(128)} %counts_ref.3) | copy-start | bytes 52
  5.0 28.7 %collective-permute-start = (bf16[37,6144]{1,0:T(8,128)(2,1)}, bf16[37,6144]{1,0:T(8,128)(2,1)S(1)}, u32[]{:S(2)}, u32[]{:S(2)}) collective-permute-start(bf16[37,6144]{1,0:T(8,128)(2,1)} %get-tuple-element.21), channel_id=1, source_target_pairs={{0,64},{64,128},{128,192},{192,256},{256,320},{320,384},{384,448},... | collective-permute-start | bytes 1363976 | tf_op jit(solution)/shard_map/ppermute | solution.py:27
  8.7 25.8 %collective-permute-start.1 = (bf16[37,6144]{1,0:T(8,128)(2,1)S(1)}, bf16[37,6144]{1,0:T(8,128)(2,1)S(1)}, u32[]{:S(2)}, u32[]{:S(2)}) collective-permute-start(bf16[37,6144]{1,0:T(8,128)(2,1)S(1)} %get-tuple-element.22), channel_id=1, source_target_pairs={{0,960},{64,0},{128,64},{192,128},{256,192},{320,256},{384,320},{4... | collective-permute-start | bytes 1363976 | tf_op jit(solution)/shard_map/ppermute | solution.py:27
  12.1 51.1 %copy-start.12 = (s32[144]{0:T(256)S(1)}, s32[144]{0:T(256)}, u32[]{:S(2)}) copy-start(s32[144]{0:T(256)} %param.7) | copy-start | bytes 1732
  12.1 49.2 %all-to-all-start = ((bf16[32,40,384]{2,1,0:T(8,128)(2,1)}), bf16[32,40,384]{2,1,0:T(8,128)(2,1)S(1)}, u32[]{:S(2)}, u32[]{:S(2)}) async-start(bf16[32,40,384]{2,1,0:T(8,128)(2,1)} %shard_map.95), calls=%async_computation | async-start | bytes 1966080 | tf_op jit(solution)/shard_map/all_to_all | solution.py:218
  33.7 0.8 copy-start.8
  34.5 0.8 copy-start.10
  35.3 1.5 %copy-start.1 = (bf16[144,6144]{1,0:T(8,128)(2,1)S(1)}, bf16[144,6144]{1,0:T(8,128)(2,1)}, u32[]{:S(2)}) copy-start(bf16[144,6144]{1,0:T(8,128)(2,1)} %patches_ref.3) | copy-start | bytes 5308420
  36.7 1.0 copy-start.9
  37.8 1.0 copy-start.11
  61.3 4.6 %collective-permute-start.2 = (bf16[32,40,384]{2,1,0:T(8,128)(2,1)S(1)}, bf16[32,40,384]{2,1,0:T(8,128)(2,1)}, u32[]{:S(2)}, u32[]{:S(2)}) collective-permute-start(bf16[32,40,384]{2,1,0:T(8,128)(2,1)S(1)} %all-to-all-done.own_ref), channel_id=1, source_target_pairs={{0,1},{1,0},{2,3},{3,2},{4,5},{5,4},{6,7},{7,6},{8,9},{9,8},{10,11... | collective-permute-start | bytes 2949128 | tf_op jit(solution)/shard_map/ppermute | solution.py:27
  70.5 4.5 %collective-permute-start.3 = (bf16[2,32,64,128]{3,2,1,0:T(8,128)(2,1)S(1)}, bf16[2,32,64,128]{3,2,1,0:T(8,128)(2,1)S(1)}, u32[]{:S(2)}, u32[]{:S(2)}) collective-permute-start(bf16[2,32,64,128]{3,2,1,0:T(8,128)(2,1)S(1)} %get-tuple-element.29), channel_id=1, source_target_pairs={{0,1},{1,0},{2,3},{3,2},{4,5},{5,4},{6,7},{7,6},{8,9},{9,8},{10,11... | collective-permute-start | bytes 3145736 | tf_op jit(solution)/shard_map/ppermute | solution.py:27
  76.5 37.8 %all-to-all-start.1 = ((bf16[64,64,128]{2,1,0:T(8,128)(2,1)}), bf16[64,64,128]{2,1,0:T(8,128)(2,1)}, u32[]{:S(2)}, u32[]{:S(2)}) async-start(bf16[64,64,128]{2,1,0:T(8,128)(2,1)} %bitcast.11), calls=%async_computation.1 | async-start | bytes 2097152 | tf_op jit(solution)/shard_map/all_to_all | solution.py:271
